TPU v7x, 32 devices: a whole 2x2x4 slice. The times are simulated.
32 devices in a mesh: bra: 8 (over z, y), ket: 4 (over x, core).
Axes of the slice: x: 2, y: 2, z: 4, core: 2. Of those that a mesh axis runs over, the one named last changes fastest.
Arguments:
- quartet_tasks: int32 [8, 4, 512, 4], P('bra', 'ket'), may hold values from 0 to 191, as said below
- factors: bfloat16 [192, 16, 128], replicated, may hold values from -4.5 to 4.5
- density: bfloat16 [192, 48, 4, 256], P('bra', None, 'ket'), may hold values from -6 to 6
Outputs:
- fock_matrix: float32 [192, 48, 4, 256], P('bra', None, 'ket')
Inputs may be any that keep to these rules, and one draw needn't show every extreme that they name: `quartet_tasks`: entries are shell numbers. On the device with bra index b and ket index k, every task's i lies among b * 24 to (b + 1) * 24 - 1 and its d has d % 4 == k. Within each half of a device's task list (the first 256 tasks and the rest), the shells c and j of all its tasks name row blocks of one bra index at most 192 times and share one remainder mod 4 at most 160 times; both bounds are reached in each half of every device's list, by the same bra index and the same remainder in both halves.
All inputs are finite; a program needn't handle non-finite values.
Results may differ from a plain program's by a relative error of at most 0.0066.
Values may be sent and summed in bfloat16 or wider, within the bound.
A program may use at most 64 MiB of HBM per device.

v0:
```python
import jax
import jax.numpy as jnp
from jax import lax
from jax.sharding import PartitionSpec as P

tile_scale = 0.0625


def pair_vectors(left_shell, right_shell):
    shell_count, basis_functions, terms = left_shell.shape
    joined = left_shell[:, :, None, :].astype(jnp.float32) * right_shell[:, None, :, :].astype(
        jnp.float32
    )
    return joined.reshape(shell_count, basis_functions * basis_functions, terms).astype(
        jnp.bfloat16
    )


def quartet_terms(factors, task_group, dens_cd, density_block_jd):
    group_member_count = task_group.shape[0]
    basis_functions = factors.shape[1]
    block_size = basis_functions * basis_functions
    bra_vec = pair_vectors(factors[task_group[:, 0]], factors[task_group[:, 1]])
    ket_vec = pair_vectors(factors[task_group[:, 2]], factors[task_group[:, 3]])
    raw_products = jnp.einsum("tpr,tqr->tpq", bra_vec, ket_vec, preferred_element_type=jnp.float32)
    integral_tile = (
        tile_scale * raw_products * lax.rsqrt(1.0 + raw_products * raw_products)
    ).astype(jnp.bfloat16)
    coulomb = jnp.einsum("tpq,tq->tp", integral_tile, dens_cd, preferred_element_type=jnp.float32)
    tile_rows = integral_tile.reshape(
        group_member_count, basis_functions, basis_functions, block_size
    ).astype(jnp.float32)
    density_rows = density_block_jd.reshape(
        group_member_count, basis_functions, basis_functions
    ).astype(jnp.float32)
    spread_rows = jnp.broadcast_to(
        density_rows[:, :, None, :],
        (group_member_count, basis_functions, basis_functions, basis_functions),
    ).reshape(group_member_count, basis_functions, block_size)
    summed_rows = jnp.sum(tile_rows * spread_rows[:, None, :, :], axis=2)
    exchange_contribution = jnp.sum(
        summed_rows.reshape(group_member_count, basis_functions, basis_functions, basis_functions),
        axis=3,
    )
    return (coulomb, exchange_contribution.reshape(group_member_count, block_size))


def evaluate(factors, quartets, dens_cd, density_block_jd):
    task_count = quartets.shape[0]
    block_size = dens_cd.shape[1]
    group_width = min(32, task_count)

    def one_group(packed):
        return quartet_terms(factors, packed[0], packed[1], packed[2])

    coulomb, exchange_contribution = lax.map(
        one_group,
        (
            quartets.reshape(-1, group_width, 4),
            dens_cd.reshape(-1, group_width, block_size),
            density_block_jd.reshape(-1, group_width, block_size),
        ),
    )
    return (
        coulomb.reshape(task_count, block_size),
        exchange_contribution.reshape(task_count, block_size),
    )


def bucket_slots(owners, count_of_owners, capacity):
    owner_marks = (owners[:, None] == jnp.arange(count_of_owners, dtype=jnp.int32)[None, :]).astype(
        jnp.int32
    )
    places = jnp.sum((jnp.cumsum(owner_marks, axis=0) - 1) * owner_marks, axis=1)
    return owners * capacity + places


def request_layout(density, shells, columns, capacity):
    bra_count = lax.axis_size("bra")
    rows_per_device, cols_dev = (density.shape[0], density.shape[1])
    owners = shells // rows_per_device
    slot_index = bucket_slots(owners, bra_count, capacity)
    wanted = shells % rows_per_device * cols_dev + columns
    asked_ids = (
        jnp.zeros((bra_count * capacity,), jnp.int32)
        .at[slot_index]
        .set(wanted)
        .reshape(bra_count, capacity)
    )
    block_table = density.reshape(rows_per_device * cols_dev, density.shape[3])
    return (slot_index, asked_ids, block_table)


def fetch_blocks(density, shells, columns, capacity):
    slot_index, asked_ids, block_table = request_layout(density, shells, columns, capacity)
    answered = lax.all_to_all(
        block_table[lax.all_to_all(asked_ids, "bra", split_axis=0, concat_axis=0, tiled=True)],
        "bra",
        split_axis=0,
        concat_axis=0,
        tiled=True,
    )
    return answered.reshape(-1, density.shape[3])[slot_index]


def body(quartet_tasks, factors, density):
    quartets = quartet_tasks.reshape(-1, 4)
    task_count = quartets.shape[0]
    bra_count = lax.axis_size("bra")
    ket_count = lax.axis_size("ket")
    rows_per_device, cols_dev, block_size = (density.shape[0], density.shape[1], density.shape[3])
    wanted_rows = jnp.stack([quartets[:, 2], quartets[:, 1]], axis=1).reshape(-1)
    wanted_cols = jnp.repeat(quartets[:, 3] // ket_count, 2)
    fetched = fetch_blocks(density, wanted_rows, wanted_cols, 6 * task_count // bra_count).reshape(
        task_count, 2, block_size
    )
    coulomb, exchange_contribution = evaluate(factors, quartets, fetched[:, 0], fetched[:, 1])
    targets = jnp.stack([quartets[:, 1], quartets[:, 2]], axis=1).reshape(-1)
    contributions = jnp.stack([coulomb, -0.5 * exchange_contribution], axis=1).reshape(
        -1, block_size
    )
    bra_rows = jnp.repeat(quartets[:, 0] % rows_per_device, 2)
    owners = targets % ket_count
    capacity = 5 * task_count // (2 * ket_count)
    slot_index = bucket_slots(owners, ket_count, capacity)
    positions = bra_rows * cols_dev + targets // ket_count
    outgoing = (
        jnp.zeros((ket_count * capacity, block_size), jnp.float32)
        .at[slot_index]
        .set(contributions)
        .reshape(ket_count, capacity, block_size)
    )
    out_index = (
        jnp.zeros((ket_count * capacity,), jnp.int32)
        .at[slot_index]
        .set(positions)
        .reshape(ket_count, capacity)
    )
    received_blocks, arrived_index = (
        lax.all_to_all(outgoing, "ket", split_axis=0, concat_axis=0, tiled=True),
        lax.all_to_all(out_index, "ket", split_axis=0, concat_axis=0, tiled=True),
    )
    fock_matrix = (
        jnp.zeros((rows_per_device * cols_dev, block_size), jnp.float32)
        .at[arrived_index.reshape(-1)]
        .add(received_blocks.reshape(-1, block_size))
    )
    return fock_matrix.reshape(rows_per_device, cols_dev, 1, block_size)


def solution(mesh):
    placed = (P("bra", "ket", None, None), P(), P("bra", None, "ket", None))
    return jax.shard_map(
        body, mesh=mesh, in_specs=placed, out_specs=P("bra", None, "ket", None), check_vma=False
    )
```

profile of v0, /device:TPU:0, one launch (start us, length us, event | category | flops | bytes accessed | tf_op | source)
XLA Modules:
  0.0 463.9 jit_solution(18255199365611753141)
XLA Ops:
  2.2 2.3 reduce-window.16
  6.1 4.3 scatter_custom_fusion.1
  10.4 13.6 %all_to_all.31 = s32[8,1,384]{2,1,0:T(1,128)S(1)} all-to-all(s32[8,1,384]{2,1,0:T(1,128)S(1)} %bitcast.126), channel_id=1, replica_groups=mesh['bra'=8,'ket'=4] {'bra'}, dimensions={0} | all-to-all | bytes 24576 | tf_op jit(solution)/shard_map/all_to_all | solution.py:97
  24.1 13.0 %gather_fusion.4 = bf16[3072,256]{1,0:T(8,128)(2,1)} fusion(bf16[1152,256]{1,0:T(8,128)(2,1)S(1)} %bitcast.111, s32[3072]{0:T(1024)S(1)} %broadcast_clamp_fusion), kind=kCustom, calls=%fused_computation.4 | custom fusion | bytes 3158016 | tf_op jit(solution)/shard_map/gather | solution.py:97
  37.1 3.7 all-to-all-start.2
  43.6 4.3 scatter_custom_fusion
  48.6 28.1 %all-to-all-done.2 = bf16[8,384,256]{2,1,0:T(8,128)(2,1)S(1)} async-done(((bf16[8,384,256]{2,1,0:T(8,128)(2,1)}), bf16[8,384,256]{2,1,0:T(8,128)(2,1)S(1)}, u32[]{:S(2)}, u32[]{:S(2)}) %all-to-all-start.2) | async-done | bytes 1572896 | tf_op jit(solution)/shard_map/all_to_all | solution.py:96
  76.7 3.4 all-to-all-start
  80.2 3.9 gather_fusion.5
  85.8 336.4 %while.12 = (s32[]{:T(128)}, f32[16,32,256]{2,1,0:T(8,128)}, f32[16,32,256]{2,1,0:T(8,128)}, s32[16,32,4]{1,0,2:T(8,128)S(1)}, bf16[192,16,128]{2,1,0:T(8,128)(2...) while((s32[]{:T(128)}, f32[16,32,256]{2,1,0:T(8,128)}, ...), condition=%wide.region_11.12_spmd, body=%wide.region_8.11_spmd.sunk | while | flops 562295168 | bytes 25054816 | solution.py:56
  89.4 1.9 multiply_convert_fusion.5
  94.9 1.9 multiply_convert_fusion.6
  98.4 5.4 %fusion.53 = (f32[32,16,256]{2,1,0:T(8,128)S(1)}, bf16[32,256,256]{2,1,0:T(8,128)(2,1)S(1)}) fusion(f32[32,16,256]{2,1,0:T(8,128)S(1)} %copy.82, bf16[32,256,128]{2,1,0:T(8,128)(2,1)} %bitcast.113, bf16[32,256,128]{2,1,0:T(8,128)(2,1)} %bitcast.114), kind=kOutput, calls=%fused_computation.11.clone.1 | convolution fusion | flops 553517056 | bytes 9437184 | tf_op jit(solution)/shard_map/while/body/eval_jaxpr/tpr,tqr->tpq/dot_general | solution.py:25
  110.4 1.9 multiply_convert_fusion.5
  115.9 1.9 multiply_convert_fusion.6
  119.5 5.4 %fusion.53 = (f32[32,16,256]{2,1,0:T(8,128)S(1)}, bf16[32,256,256]{2,1,0:T(8,128)(2,1)S(1)}) fusion(f32[32,16,256]{2,1,0:T(8,128)S(1)} %copy.82, bf16[32,256,128]{2,1,0:T(8,128)(2,1)} %bitcast.113, bf16[32,256,128]{2,1,0:T(8,128)(2,1)} %bitcast.114), kind=kOutput, calls=%fused_computation.11.clone.1 | convolution fusion | flops 553517056 | bytes 9437184 | tf_op jit(solution)/shard_map/while/body/eval_jaxpr/tpr,tqr->tpq/dot_general | solution.py:25
  131.4 1.9 multiply_convert_fusion.5
  136.9 1.9 multiply_convert_fusion.6
  140.5 5.4 %fusion.53 = (f32[32,16,256]{2,1,0:T(8,128)S(1)}, bf16[32,256,256]{2,1,0:T(8,128)(2,1)S(1)}) fusion(f32[32,16,256]{2,1,0:T(8,128)S(1)} %copy.82, bf16[32,256,128]{2,1,0:T(8,128)(2,1)} %bitcast.113, bf16[32,256,128]{2,1,0:T(8,128)(2,1)} %bitcast.114), kind=kOutput, calls=%fused_computation.11.clone.1 | convolution fusion | flops 553517056 | bytes 9437184 | tf_op jit(solution)/shard_map/while/body/eval_jaxpr/tpr,tqr->tpq/dot_general | solution.py:25
  152.5 1.9 multiply_convert_fusion.5
  157.9 1.9 multiply_convert_fusion.6
  161.5 5.4 %fusion.53 = (f32[32,16,256]{2,1,0:T(8,128)S(1)}, bf16[32,256,256]{2,1,0:T(8,128)(2,1)S(1)}) fusion(f32[32,16,256]{2,1,0:T(8,128)S(1)} %copy.82, bf16[32,256,128]{2,1,0:T(8,128)(2,1)} %bitcast.113, bf16[32,256,128]{2,1,0:T(8,128)(2,1)} %bitcast.114), kind=kOutput, calls=%fused_computation.11.clone.1 | convolution fusion | flops 553517056 | bytes 9437184 | tf_op jit(solution)/shard_map/while/body/eval_jaxpr/tpr,tqr->tpq/dot_general | solution.py:25
  173.5 1.9 multiply_convert_fusion.5
  179.0 1.9 multiply_convert_fusion.6
  182.5 5.4 %fusion.53 = (f32[32,16,256]{2,1,0:T(8,128)S(1)}, bf16[32,256,256]{2,1,0:T(8,128)(2,1)S(1)}) fusion(f32[32,16,256]{2,1,0:T(8,128)S(1)} %copy.82, bf16[32,256,128]{2,1,0:T(8,128)(2,1)} %bitcast.113, bf16[32,256,128]{2,1,0:T(8,128)(2,1)} %bitcast.114), kind=kOutput, calls=%fused_computation.11.clone.1 | convolution fusion | flops 553517056 | bytes 9437184 | tf_op jit(solution)/shard_map/while/body/eval_jaxpr/tpr,tqr->tpq/dot_general | solution.py:25
  194.5 1.9 multiply_convert_fusion.5
  200.0 1.9 multiply_convert_fusion.6
  203.6 5.4 %fusion.53 = (f32[32,16,256]{2,1,0:T(8,128)S(1)}, bf16[32,256,256]{2,1,0:T(8,128)(2,1)S(1)}) fusion(f32[32,16,256]{2,1,0:T(8,128)S(1)} %copy.82, bf16[32,256,128]{2,1,0:T(8,128)(2,1)} %bitcast.113, bf16[32,256,128]{2,1,0:T(8,128)(2,1)} %bitcast.114), kind=kOutput, calls=%fused_computation.11.clone.1 | convolution fusion | flops 553517056 | bytes 9437184 | tf_op jit(solution)/shard_map/while/body/eval_jaxpr/tpr,tqr->tpq/dot_general | solution.py:25
  215.5 1.9 multiply_convert_fusion.5
  221.0 1.9 multiply_convert_fusion.6
  224.6 5.4 %fusion.53 = (f32[32,16,256]{2,1,0:T(8,128)S(1)}, bf16[32,256,256]{2,1,0:T(8,128)(2,1)S(1)}) fusion(f32[32,16,256]{2,1,0:T(8,128)S(1)} %copy.82, bf16[32,256,128]{2,1,0:T(8,128)(2,1)} %bitcast.113, bf16[32,256,128]{2,1,0:T(8,128)(2,1)} %bitcast.114), kind=kOutput, calls=%fused_computation.11.clone.1 | convolution fusion | flops 553517056 | bytes 9437184 | tf_op jit(solution)/shard_map/while/body/eval_jaxpr/tpr,tqr->tpq/dot_general | solution.py:25
  236.6 1.9 multiply_convert_fusion.5
  242.0 1.9 multiply_convert_fusion.6
  245.6 5.4 %fusion.53 = (f32[32,16,256]{2,1,0:T(8,128)S(1)}, bf16[32,256,256]{2,1,0:T(8,128)(2,1)S(1)}) fusion(f32[32,16,256]{2,1,0:T(8,128)S(1)} %copy.82, bf16[32,256,128]{2,1,0:T(8,128)(2,1)} %bitcast.113, bf16[32,256,128]{2,1,0:T(8,128)(2,1)} %bitcast.114), kind=kOutput, calls=%fused_computation.11.clone.1 | convolution fusion | flops 553517056 | bytes 9437184 | tf_op jit(solution)/shard_map/while/body/eval_jaxpr/tpr,tqr->tpq/dot_general | solution.py:25
  257.6 1.9 multiply_convert_fusion.5
  263.0 1.9 multiply_convert_fusion.6
  266.6 5.4 %fusion.53 = (f32[32,16,256]{2,1,0:T(8,128)S(1)}, bf16[32,256,256]{2,1,0:T(8,128)(2,1)S(1)}) fusion(f32[32,16,256]{2,1,0:T(8,128)S(1)} %copy.82, bf16[32,256,128]{2,1,0:T(8,128)(2,1)} %bitcast.113, bf16[32,256,128]{2,1,0:T(8,128)(2,1)} %bitcast.114), kind=kOutput, calls=%fused_computation.11.clone.1 | convolution fusion | flops 553517056 | bytes 9437184 | tf_op jit(solution)/shard_map/while/body/eval_jaxpr/tpr,tqr->tpq/dot_general | solution.py:25
  278.6 1.9 multiply_convert_fusion.5
  284.1 1.9 multiply_convert_fusion.6
  287.7 5.4 %fusion.53 = (f32[32,16,256]{2,1,0:T(8,128)S(1)}, bf16[32,256,256]{2,1,0:T(8,128)(2,1)S(1)}) fusion(f32[32,16,256]{2,1,0:T(8,128)S(1)} %copy.82, bf16[32,256,128]{2,1,0:T(8,128)(2,1)} %bitcast.113, bf16[32,256,128]{2,1,0:T(8,128)(2,1)} %bitcast.114), kind=kOutput, calls=%fused_computation.11.clone.1 | convolution fusion | flops 553517056 | bytes 9437184 | tf_op jit(solution)/shard_map/while/body/eval_jaxpr/tpr,tqr->tpq/dot_general | solution.py:25
  299.6 1.9 multiply_convert_fusion.5
  305.1 1.9 multiply_convert_fusion.6
  308.7 5.4 %fusion.53 = (f32[32,16,256]{2,1,0:T(8,128)S(1)}, bf16[32,256,256]{2,1,0:T(8,128)(2,1)S(1)}) fusion(f32[32,16,256]{2,1,0:T(8,128)S(1)} %copy.82, bf16[32,256,128]{2,1,0:T(8,128)(2,1)} %bitcast.113, bf16[32,256,128]{2,1,0:T(8,128)(2,1)} %bitcast.114), kind=kOutput, calls=%fused_computation.11.clone.1 | convolution fusion | flops 553517056 | bytes 9437184 | tf_op jit(solution)/shard_map/while/body/eval_jaxpr/tpr,tqr->tpq/dot_general | solution.py:25
  320.7 1.9 multiply_convert_fusion.5
  326.1 1.9 multiply_convert_fusion.6
  329.7 5.4 %fusion.53 = (f32[32,16,256]{2,1,0:T(8,128)S(1)}, bf16[32,256,256]{2,1,0:T(8,128)(2,1)S(1)}) fusion(f32[32,16,256]{2,1,0:T(8,128)S(1)} %copy.82, bf16[32,256,128]{2,1,0:T(8,128)(2,1)} %bitcast.113, bf16[32,256,128]{2,1,0:T(8,128)(2,1)} %bitcast.114), kind=kOutput, calls=%fused_computation.11.clone.1 | convolution fusion | flops 553517056 | bytes 9437184 | tf_op jit(solution)/shard_map/while/body/eval_jaxpr/tpr,tqr->tpq/dot_general | solution.py:25
  341.7 1.9 multiply_convert_fusion.5
  347.1 1.9 multiply_convert_fusion.6
  350.7 5.4 %fusion.53 = (f32[32,16,256]{2,1,0:T(8,128)S(1)}, bf16[32,256,256]{2,1,0:T(8,128)(2,1)S(1)}) fusion(f32[32,16,256]{2,1,0:T(8,128)S(1)} %copy.82, bf16[32,256,128]{2,1,0:T(8,128)(2,1)} %bitcast.113, bf16[32,256,128]{2,1,0:T(8,128)(2,1)} %bitcast.114), kind=kOutput, calls=%fused_computation.11.clone.1 | convolution fusion | flops 553517056 | bytes 9437184 | tf_op jit(solution)/shard_map/while/body/eval_jaxpr/tpr,tqr->tpq/dot_general | solution.py:25
  362.7 1.9 multiply_convert_fusion.5
  368.2 1.9 multiply_convert_fusion.6
  371.7 5.4 %fusion.53 = (f32[32,16,256]{2,1,0:T(8,128)S(1)}, bf16[32,256,256]{2,1,0:T(8,128)(2,1)S(1)}) fusion(f32[32,16,256]{2,1,0:T(8,128)S(1)} %copy.82, bf16[32,256,128]{2,1,0:T(8,128)(2,1)} %bitcast.113, bf16[32,256,128]{2,1,0:T(8,128)(2,1)} %bitcast.114), kind=kOutput, calls=%fused_computation.11.clone.1 | convolution fusion | flops 553517056 | bytes 9437184 | tf_op jit(solution)/shard_map/while/body/eval_jaxpr/tpr,tqr->tpq/dot_general | solution.py:25
  383.7 1.9 multiply_convert_fusion.5
  389.2 1.9 multiply_convert_fusion.6
  392.8 5.4 %fusion.53 = (f32[32,16,256]{2,1,0:T(8,128)S(1)}, bf16[32,256,256]{2,1,0:T(8,128)(2,1)S(1)}) fusion(f32[32,16,256]{2,1,0:T(8,128)S(1)} %copy.82, bf16[32,256,128]{2,1,0:T(8,128)(2,1)} %bitcast.113, bf16[32,256,128]{2,1,0:T(8,128)(2,1)} %bitcast.114), kind=kOutput, calls=%fused_computation.11.clone.1 | convolution fusion | flops 553517056 | bytes 9437184 | tf_op jit(solution)/shard_map/while/body/eval_jaxpr/tpr,tqr->tpq/dot_general | solution.py:25
  401.2 1.7 gather_fusion
  404.8 1.9 multiply_convert_fusion.5
  410.2 1.9 multiply_convert_fusion.6
  413.8 5.4 %fusion.53 = (f32[32,16,256]{2,1,0:T(8,128)S(1)}, bf16[32,256,256]{2,1,0:T(8,128)(2,1)S(1)}) fusion(f32[32,16,256]{2,1,0:T(8,128)S(1)} %copy.82, bf16[32,256,128]{2,1,0:T(8,128)(2,1)} %bitcast.113, bf16[32,256,128]{2,1,0:T(8,128)(2,1)} %bitcast.114), kind=kOutput, calls=%fused_computation.11.clone.1 | convolution fusion | flops 553517056 | bytes 9437184 | tf_op jit(solution)/shard_map/while/body/eval_jaxpr/tpr,tqr->tpq/dot_general | solution.py:25
  426.0 6.1 %scatter_custom_fusion.2 = f32[1280,256]{1,0:T(8,128)} fusion(s32[1024]{0:T(1024)S(1)} %bitcast.137, f32[1024,256]{1,0:T(8,128)S(1)} %reshape.467, f32[]{:T(128)} %constant.98.clone.1), kind=kCustom, calls=%fused_computation.36 | custom fusion | bytes 1310724 | tf_op jit(solution)/shard_map/scatter | solution.py:130
  432.1 3.5 all-to-all-start.3
  435.8 17.1 %all-to-all-done.3 = f32[4,320,256]{2,1,0:T(8,128)S(1)} async-done(((f32[4,320,256]{2,1,0:T(8,128)}), f32[4,320,256]{2,1,0:T(8,128)S(1)}, u32[]{:S(2)}, u32[]{:S(2)}) %all-to-all-start.3) | async-done | bytes 1310752 | tf_op jit(solution)/shard_map/all_to_all | solution.py:140
  452.9 8.8 %scatter_custom_fusion.3 = f32[1152,256]{1,0:T(8,128)S(1)} fusion(s32[1280]{0:T(1024)S(1)} %fusion.19, f32[1280,256]{1,0:T(8,128)S(1)} %bitcast.120, f32[]{:T(128)} %constant.98.clone.1), kind=kCustom, calls=%fused_computation.38 | custom fusion | flops 327680 | bytes 1179652 | tf_op jit(solution)/shard_map/scatter-add | solution.py:146
  461.7 2.2 reshape.396
  (448 shorter events, 198.9 us)
Async XLA Ops:
  0.0 24.1 %copy-start = (bf16[24,48,1,256]{3,1,2,0:T(8,128)(2,1)S(1)}, bf16[24,48,1,256]{3,1,2,0:T(8,128)(2,1)}, u32[]{:S(2)}) copy-start(bf16[24,48,1,256]{3,1,2,0:T(8,128)(2,1)} %param.7) | copy-start | bytes 1769476
  37.1 3.7 copy-start.1
  37.1 39.7 %all-to-all-start.2 = ((bf16[8,384,256]{2,1,0:T(8,128)(2,1)}), bf16[8,384,256]{2,1,0:T(8,128)(2,1)S(1)}, u32[]{:S(2)}, u32[]{:S(2)}) async-start(bf16[8,384,256]{2,1,0:T(8,128)(2,1)} %bitcast.118), calls=%async_computation.2 | async-start | bytes 3145728 | tf_op jit(solution)/shard_map/all_to_all | solution.py:96
  76.7 355.3 %all-to-all-start = ((s32[4,1,320]{2,1,0:T(1,128)}), s32[4,1,320]{2,1,0:T(1,128)S(1)}, u32[]{:S(2)}, u32[]{:S(2)}) async-start(s32[4,1,320]{2,1,0:T(1,128)} %all_to_all.20), calls=%async_computation | async-start | bytes 12288 | tf_op jit(solution)/shard_map/all_to_all | solution.py:141
  432.1 20.8 %all-to-all-start.3 = ((f32[4,320,256]{2,1,0:T(8,128)}), f32[4,320,256]{2,1,0:T(8,128)S(1)}, u32[]{:S(2)}, u32[]{:S(2)}) async-start(f32[4,320,256]{2,1,0:T(8,128)} %bitcast.35), calls=%async_computation.3 | async-start | bytes 2621440 | tf_op jit(solution)/shard_map/all_to_all | solution.py:140
where the time goes:
time: 468 us; the launch traced here: 464 us
  local copies, waits for them, and re-layouts  201 us (43%)
  matrix products  105 us (22%)
  other arithmetic  86.5 us (18%)
  waiting for transfers between devices  45.2 us (10%)
  blocking collectives  13.6 us (3%)
  starting transfers between devices  10.7 us (2%)
    dot_general x16, matrix products, quartet_terms(): jnp.einsum('tpr,tqr->tpq', bra_vec, ket_vec, preferred_element_type=jnp.f...  85.9 us
    convert_element_type x32, other arithmetic, pair_vectors(): joined.reshape(shell_count, basis_functions * basis_functions, terms)  60.9 us
    gather x32, local copies, waits for them, and re-layouts, quartet_terms(): bra_vec = pair_vectors(factors[task_group[:, 0]], factors[task_group[:, 1]])  55.2 us
    gather x32, local copies, waits for them, and re-layouts, quartet_terms(): ket_vec = pair_vectors(factors[task_group[:, 2]], factors[task_group[:, 3]])  55.2 us
    all_to_all x1, waiting for transfers between devices, fetch_blocks(): lax.all_to_all(block_table[lax.all_to_all(asked_ids, 'bra', split_axis=0,...  28.1 us
    dot_general x16, matrix products, quartet_terms(): jnp.einsum('tpq,tq->tp', integral_tile, dens_cd, preferred_element_type=j...  18.8 us
    all_to_all x1, waiting for transfers between devices, body(): lax.all_to_all(outgoing, 'ket', split_axis=0, concat_axis=0, tiled=True)  17.1 us
    all_to_all x1, blocking collectives, fetch_blocks(): lax.all_to_all(asked_ids, 'bra', split_axis=0, concat_axis=0, tiled=True)  13.6 us
  transfers between devices with their start and end apart: 3, of which 2 were waited for; matrix products, arithmetic and copies ran while one was open for 77% of the time, Pallas kernels for 0%

commit v1 on v0

v1 whole, which is shorter than its diff:
```python
import functools

import jax
import jax.numpy as jnp
from jax import lax
from jax.experimental import pallas as pl
from jax.experimental.pallas import tpu as pltpu
from jax.sharding import PartitionSpec as P

tile_scale = 0.0625
NT = (((1,), (1,)), ((), ()))
NN = (((1,), (0,)), ((), ()))
VMEM = pl.BlockSpec(memory_space=pltpu.VMEM)
SMEM = pl.BlockSpec(memory_space=pltpu.SMEM)
PARAMS = pltpu.CompilerParams(vmem_limit_bytes=48 * 1024 * 1024)


def iota(shape, axis):
    return lax.broadcasted_iota(jnp.int32, shape, axis)


def dot(left, right, dims):
    return lax.dot_general(left, right, dims, preferred_element_type=jnp.float32)


def hot(mask):
    return jnp.where(mask, 1.0, 0.0).astype(jnp.bfloat16)


def plan_kernel(sides, bucket_refs, wanted_refs, slot_refs, asked_refs):
    items = bucket_refs[0].shape[1]
    upper = hot(iota((items, items), 0) <= iota((items, items), 1))
    for side, (buckets, capacity) in enumerate(sides):
        owner_id = iota((buckets, items), 0)
        marked = jnp.where(bucket_refs[side][...] == owner_id, 1.0, 0.0)
        counted = dot(marked.astype(jnp.bfloat16), upper, NN)
        offset = (owner_id * capacity - 1).astype(jnp.float32)
        slot = jnp.sum(marked * (counted + offset), axis=0, keepdims=True).astype(jnp.int32)
        slot_refs[side][...] = slot
        wanted = wanted_refs[side][...]
        which = iota((16, items), 0)
        high, low = wanted >> 6, wanted & 63
        values = jnp.where(which == 0, high, jnp.where(which == 1, low, 0))
        values = values.astype(jnp.float32).astype(jnp.bfloat16)
        width = 256

        def part(k, carry, side=side, slot=slot, values=values):
            first = pl.multiple_of(k * width, width)
            picked = hot(slot == iota((width, items), 0) + first)
            found = dot(values, picked, NT)
            asked_refs[side][:, pl.ds(first, width)] = (
                found[0:1] * 64.0 + found[1:2]
            ).astype(jnp.int32)
            return carry

        lax.fori_loop(0, buckets * capacity // width, part, 0)


def plan(buckets, wanted, sides):
    count = len(sides)
    items = buckets[0].shape[1]

    def kernel(*refs):
        plan_kernel(
            sides,
            refs[:count],
            refs[count : 2 * count],
            refs[2 * count : 3 * count],
            refs[3 * count :],
        )

    out = pl.pallas_call(
        kernel,
        out_shape=[jax.ShapeDtypeStruct((1, items), jnp.int32)] * count
        + [jax.ShapeDtypeStruct((1, b * c), jnp.int32) for b, c in sides],
        in_specs=[VMEM] * (2 * count),
        out_specs=[VMEM] * (2 * count),
        compiler_params=PARAMS,
        name="plan",
    )(*buckets, *wanted)
    return out[:count], out[count:]


def serve_kernel(ids_ref, table_ref, out_ref):
    rows = ids_ref.shape[1]
    blocks = table_ref.shape[0]
    spread = jnp.broadcast_to(ids_ref[...], (128, rows)).T
    spread = jnp.concatenate([spread] * (blocks // 128), axis=1)
    picked = hot(spread == iota((rows, blocks), 1))
    out_ref[...] = dot(picked, table_ref[...], NN).astype(jnp.bfloat16)


def serve(ids, table):
    wide = 256
    total = ids.shape[1]
    return pl.pallas_call(
        serve_kernel,
        grid=(total // wide,),
        out_shape=jax.ShapeDtypeStruct((total, table.shape[1]), jnp.bfloat16),
        in_specs=[
            pl.BlockSpec((1, wide), lambda k: (0, k)),
            pl.BlockSpec(table.shape, lambda k: (0, 0)),
        ],
        out_specs=pl.BlockSpec((wide, table.shape[1]), lambda k: (k, 0)),
        compiler_params=PARAMS,
        cost_estimate=pl.CostEstimate(
            flops=2 * total * table.shape[0] * table.shape[1],
            bytes_accessed=4 * total * table.shape[1],
            transcendentals=0,
        ),
        name="serve",
    )(ids, table)


def pair_rows(slow_ref, slow, fast):
    funcs = fast.shape[0]
    parts = []
    for at in range(funcs):
        row = jnp.broadcast_to(slow_ref[slow, at : at + 1, :], fast.shape).astype(jnp.bfloat16)
        parts.append(row * fast)
    return jnp.concatenate(parts, axis=0)


def task_kernel(
    tasks_ref, slots_ref, places_ref, fac_ref, got_ref, out_ref,
    fac32, got32, dens, spread, dens_cd, partial, coulomb, routed, unroll,
):
    shells, funcs, terms = fac_ref.shape
    size = funcs * funcs
    count = spread.shape[1]
    fac32[...] = fac_ref[...].astype(jnp.float32)
    got32[...] = got_ref[...].astype(jnp.float32)

    def gather(t, carry):
        for side in range(2):
            dens[side, pl.ds(t, 1), :] = got32[pl.ds(slots_ref[2 * t + side], 1), :]
        return carry

    lax.fori_loop(0, count, gather, 0, unroll=8)
    row, col = iota((size, size), 0), iota((size, size), 1)
    row_hi, row_lo, col_hi, col_lo = row // funcs, row % funcs, col // funcs, col % funcs
    swap = hot((row_hi == col_lo) & (row_lo == col_hi))
    dens_cd[...] = dot(dens[0].astype(jnp.bfloat16), swap, NN)
    dens_jd = dens[1].astype(jnp.bfloat16)

    def spread_one(f, carry):
        spread[f] = dot(dens_jd, hot((row_hi == col_lo) & (row_lo == f)), NN)
        return carry

    lax.fori_loop(0, funcs, spread_one, 0)

    def one_task(t):
        shell_i, shell_j = tasks_ref[4 * t], tasks_ref[4 * t + 1]
        shell_c, shell_d = tasks_ref[4 * t + 2], tasks_ref[4 * t + 3]
        ket = pair_rows(fac32, shell_d, fac_ref[shell_c])
        bra = pair_rows(fac32, shell_i, fac_ref[shell_j])
        raw = dot(ket, bra, NT)
        tile = raw * lax.rsqrt(1.0 + raw * raw)
        total = None
        for f in range(funcs):
            term = tile[f * funcs : (f + 1) * funcs] * spread[f, pl.ds(t, 1), :]
            total = term if total is None else total + term
        place = pl.ds(pl.multiple_of(t * funcs, funcs), funcs)
        for lane in range(size // 128):
            partial[lane, place, :] = total[:, lane * 128 : (lane + 1) * 128]
        weights = jnp.broadcast_to(dens_cd[pl.ds(t, 1), :], (16, size)).astype(jnp.bfloat16)
        summed = dot(weights, tile.astype(jnp.bfloat16), NN)
        coulomb[pl.ds(t, 1), :] = summed[0:1]

    def some_tasks(step, carry):
        for k in range(unroll):
            one_task(step * unroll + k)
        return carry

    lax.fori_loop(0, count // unroll, some_tasks, 0)

    dens[0] = coulomb[...] * tile_scale
    dens[1] = jnp.zeros((count, size), jnp.float32)

    def fold(e, carry):
        picked = pl.ds(e, count, stride=funcs)
        rows = [partial[lane, picked, :] for lane in range(size // 128)]
        rows = jnp.concatenate(rows, axis=1).astype(jnp.bfloat16)
        dens[1] += dot(rows, hot((row_hi == col_hi) & (col_lo == e)), NN)
        return carry

    lax.fori_loop(0, funcs, fold, 0)
    dens[1] = dens[1] * (-0.5 * tile_scale)
    routed[...] = jnp.zeros_like(routed)

    def route(t, carry):
        for side in range(2):
            routed[pl.ds(places_ref[2 * t + side], 1), :] = dens[side, pl.ds(t, 1), :]
        return carry

    lax.fori_loop(0, count, route, 0, unroll=8)
    out_ref[...] = routed[...].astype(jnp.bfloat16)


def run_tasks(tasks, slots, places, factors, got, out_rows, unroll):
    count = tasks.shape[0] // 4
    shells, funcs, terms = factors.shape
    size = funcs * funcs
    f32 = jnp.float32
    return pl.pallas_call(
        functools.partial(task_kernel, unroll=unroll),
        out_shape=jax.ShapeDtypeStruct((out_rows, size), jnp.bfloat16),
        in_specs=[SMEM, SMEM, SMEM, VMEM, VMEM],
        out_specs=VMEM,
        scratch_shapes=[
            pltpu.VMEM((shells, funcs, terms), f32),
            pltpu.VMEM(got.shape, f32),
            pltpu.VMEM((2, count, size), f32),
            pltpu.VMEM((funcs, count, size), f32),
            pltpu.VMEM((count, size), f32),
            pltpu.VMEM((size // 128, count * funcs, 128), f32),
            pltpu.VMEM((count, size), f32),
            pltpu.VMEM((out_rows, size), f32),
        ],
        compiler_params=PARAMS,
        cost_estimate=pl.CostEstimate(
            flops=16 * count * size * size * terms,
            bytes_accessed=2 * shells * funcs * terms,
            transcendentals=count * size * size,
        ),
        name="tasks",
    )(tasks, slots, places, factors, got)


def sum_kernel(index_a, index_b, block_a, block_b, out_ref):
    rows = out_ref.shape[0]
    first = pl.program_id(0) * rows
    total = None
    for index, block in ((index_a, block_a), (index_b, block_b)):
        picked = hot(index[...] == iota((rows, index.shape[1]), 0) + first)
        term = dot(picked, block[...], NN)
        total = term if total is None else total + term
    out_ref[...] = total


def sum_blocks(indices, blocks, total):
    rows = 128
    size = blocks[0].shape[1]
    whole = lambda array: pl.BlockSpec(array.shape, lambda k: (0, 0))
    return pl.pallas_call(
        sum_kernel,
        grid=(total // rows,),
        out_shape=jax.ShapeDtypeStruct((total, size), jnp.float32),
        in_specs=[whole(indices[0]), whole(indices[1]), whole(blocks[0]), whole(blocks[1])],
        out_specs=pl.BlockSpec((rows, size), lambda k: (k, 0)),
        compiler_params=PARAMS,
        name="sum_blocks",
    )(*indices, *blocks)


def trade(array, axis):
    return lax.all_to_all(array, axis, split_axis=0, concat_axis=0, tiled=True)


def body(quartet_tasks, factors, density):
    quartets = quartet_tasks.reshape(-1, 4)
    task_count = quartets.shape[0]
    half = task_count // 2
    bra_count = lax.axis_size("bra")
    ket_count = lax.axis_size("ket")
    rows_per_device, cols_dev, size = (density.shape[0], density.shape[1], density.shape[3])
    table = density.reshape(rows_per_device * cols_dev, size)
    shell_i, shell_j, shell_c, shell_d = (quartets[:, k] for k in range(4))

    cap_bra = 3 * task_count // bra_count
    cap_ket = 5 * task_count // (4 * ket_count)
    half_of = jnp.arange(2 * task_count, dtype=jnp.int32) // task_count
    wanted_shell = jnp.stack([shell_c, shell_j], axis=1).reshape(-1)
    wanted = wanted_shell % rows_per_device * cols_dev + jnp.repeat(shell_d // ket_count, 2)
    bra_bucket = wanted_shell // rows_per_device * 2 + half_of
    target = jnp.stack([shell_j, shell_c], axis=1).reshape(-1)
    position = jnp.repeat(shell_i % rows_per_device, 2) * cols_dev + target // ket_count
    ket_bucket = target % ket_count * 2 + half_of
    slots, asked = plan(
        [bra_bucket[None], ket_bucket[None]],
        [wanted[None], position[None]],
        ((2 * bra_count, cap_bra), (2 * ket_count, cap_ket)),
    )
    asked_bra = trade(asked[0].reshape(bra_count, 2 * cap_bra), "bra")
    asked_bra = asked_bra.reshape(bra_count, 2, cap_bra).transpose(1, 0, 2)
    arrived = trade(asked[1].reshape(ket_count, 2 * cap_ket), "ket")
    arrived = arrived.reshape(ket_count, 2, cap_ket).transpose(1, 0, 2)

    def per_half(slot, capacity, which):
        bucket, place = slot // capacity, slot % capacity
        local = bucket // 2 * capacity + place
        return local[which * task_count : (which + 1) * task_count]

    results = []
    for which in range(2):
        served = serve(asked_bra[which].reshape(1, -1), table)
        got = trade(served.reshape(bra_count, cap_bra, size), "bra")
        outgoing = run_tasks(
            quartets[which * half : (which + 1) * half].reshape(-1),
            per_half(slots[0].reshape(-1), cap_bra, which),
            per_half(slots[1].reshape(-1), cap_ket, which),
            factors,
            got.reshape(-1, size),
            ket_count * cap_ket,
            4,
        )
        back = trade(outgoing.reshape(ket_count, cap_ket, size), "ket")
        results.append(back.reshape(-1, size))
    fock = sum_blocks(
        [arrived[0].reshape(1, -1), arrived[1].reshape(1, -1)],
        results,
        rows_per_device * cols_dev,
    )
    return fock.reshape(rows_per_device, cols_dev, 1, size)


def solution(mesh):
    placed = (P("bra", "ket", None, None), P(), P("bra", None, "ket", None))
    return jax.shard_map(
        body, mesh=mesh, in_specs=placed, out_specs=P("bra", None, "ket", None), check_vma=False
    )
```

time: 468 us -> 234 us (0.50)
  local copies, waits for them, and re-layouts: 201 us -> 6.68 us
  Pallas kernels: 0 us -> 172 us
  matrix products: 105 us -> 0 us
  other arithmetic: 86.5 us -> 1.17 us
  waiting for transfers between devices: 45.2 us -> 28.8 us
  starting transfers between devices: 10.7 us -> 24.7 us
  blocking collectives: 13.6 us -> 0 us
    pallas_call x0 -> x6, Pallas kernels: none -> 172 us  [the longest x2 156 us: run_tasks(): pl.pallas_call(functools.partial(task_kernel, unroll=unroll), out_shape=j...]
    gather x66 -> x0, local copies, waits for them, and re-layouts: 127 us -> none  [the longest x32 55.2 us: quartet_terms(): bra_vec = pair_vectors(factors[task_group[:, 0]], factors[task_group[:, 1]])]
    dot_general x32 -> x0, matrix products: 105 us -> none  [the longest x16 85.9 us: quartet_terms(): jnp.einsum('tpr,tqr->tpq', bra_vec, ket_vec, preferred_element_type=jnp.f...]
    convert_element_type x98 -> x0, other arithmetic: 62.2 us -> none  [the longest x32 60.9 us: pair_vectors(): joined.reshape(shell_count, basis_functions * basis_functions, terms)]
    all_to_all x3 -> x6, waiting for transfers between devices: 45.2 us -> 28.8 us  [trade(): return lax.all_to_all(array, axis, split_axis=0, concat_axis=0, tiled=True)]
    scatter x3 -> x0, local copies, waits for them, and re-layouts: 14.8 us -> none  [the longest x1 6.11 us: body(): outgoing = jnp.zeros((ket_count * capacity, block_size), jnp.float32).at[...]
    all_to_all x3 -> x6, starting transfers between devices: 10.7 us -> 24.7 us  [trade(): return lax.all_to_all(array, axis, split_axis=0, concat_axis=0, tiled=True)]
    all_to_all x1 -> x0, blocking collectives: 13.6 us -> none  [fetch_blocks(): lax.all_to_all(asked_ids, 'bra', split_axis=0, concat_axis=0, tiled=True)]
  transfers between devices with their start and end apart: 3 -> 6, of which waited for: 2 -> 3; matrix products, arithmetic and copies ran while one was open for 77% -> 1% of each run, Pallas kernels for 0% -> 70%
where the time goes in v1:
time: 234 us; the launch traced here: 233 us
  Pallas kernels  172 us (74%)
  waiting for transfers between devices  28.8 us (12%)
  starting transfers between devices  24.7 us (11%)
  local copies, waits for them, and re-layouts  6.68 us (3%)
    pallas_call x2, Pallas kernels, run_tasks(): pl.pallas_call(functools.partial(task_kernel, unroll=unroll), out_shape=j...  156 us
    all_to_all x6, waiting for transfers between devices, trade(): return lax.all_to_all(array, axis, split_axis=0, concat_axis=0, tiled=True)  28.8 us
    all_to_all x6, starting transfers between devices, trade(): return lax.all_to_all(array, axis, split_axis=0, concat_axis=0, tiled=True)  24.7 us
    pallas_call x2, Pallas kernels, serve(): pl.pallas_call(serve_kernel, grid=(total // wide,), out_shape=jax.ShapeDt...  7.37 us
    pallas_call x1, Pallas kernels, plan(): pl.pallas_call(kernel, out_shape=[jax.ShapeDtypeStruct((1, items), jnp.in...  5.6 us
  transfers between devices with their start and end apart: 6, of which 3 were waited for; matrix products, arithmetic and copies ran while one was open for 1% of the time, Pallas kernels for 70%

profile of v1, /device:TPU:0, one launch (start us, length us, event | category | flops | bytes accessed | tf_op | source)
XLA Modules:
  0.0 233.2 jit_solution(13394748250010011067)
XLA Ops:
  0.0 0.7 stack.8
  0.7 0.9 slice_remainder_fusion
  1.6 0.2 copy.16
  1.8 0.2 ne.217
  2.0 0.1 copy.17
  2.2 0.2 rem.156
  2.4 0.0 copy-start.1
  2.4 0.1 copy.19
  2.5 0.2 reshape.331
  2.7 0.1 broadcast_in_dim.4
  2.8 0.2 reshape.332
  3.0 0.1 broadcast_in_dim.5
  3.2 0.2 mul.56
  3.3 0.1 copy.18
  3.5 0.2 div.83
  3.8 5.6 %plan.1 = (s32[1,1024]{1,0:T(1,128)S(1)}, s32[1,1024]{1,0:T(1,128)S(1)}, s32[1,3072]{1,0:T(1,128)}, s32[1,1280]{1,0:T(1,128)S(1)}) custom-call(s32[1,1024]{1,0:T(1,128)S(1)} %get-tuple-element.34.refs_0_, s32[1,1024]{1,0:T(1,128)S(1)} %get-tuple-element.32.refs_1_, s32[1,1024]{1,0:T(1,128)S(1)} %get-tuple-element.33.refs_2_, ...), custom_call_target="tpu_custom_call" | custom-call | tf_op jit(solution)/shard_map/plan/pallas_call | solution.py:72
  9.4 7.3 %all-to-all-start.1 = ((s32[8,1,384]{2,1,0:T(1,128)}), s32[8,1,384]{2,1,0:T(1,128)S(1)}, u32[]{:S(2)}, u32[]{:S(2)}) async-start(s32[8,1,384]{2,1,0:T(1,128)} %bitcast.8), calls=%async_computation.1 | async-start | bytes 24576 | tf_op jit(solution)/shard_map/all_to_all | solution.py:257
  16.7 0.7 all_to_all.32
  17.3 5.9 %all-to-all-done.1 = s32[8,1,384]{2,1,0:T(1,128)S(1)} async-done(((s32[8,1,384]{2,1,0:T(1,128)}), s32[8,1,384]{2,1,0:T(1,128)S(1)}, u32[]{:S(2)}, u32[]{:S(2)}) %all-to-all-start.1) | async-done | bytes 12320 | tf_op jit(solution)/shard_map/all_to_all | solution.py:257
  23.2 3.2 %all-to-all-start = ((s32[4,1,320]{2,1,0:T(1,128)}), s32[4,1,320]{2,1,0:T(1,128)S(1)}, u32[]{:S(2)}, u32[]{:S(2)}) async-start(s32[4,1,320]{2,1,0:T(1,128)} %all_to_all.32), calls=%async_computation | async-start | bytes 12288 | tf_op jit(solution)/shard_map/all_to_all | solution.py:257
  26.5 0.1 reshape.335
  26.6 0.1 reshape_squeeze.14.ids_ref
  26.7 0.0 copy-done.1
  26.7 3.7 %serve.2 = bf16[1536,256]{1,0:T(8,128)(2,1)} custom-call(s32[1,1536]{1,0:T(1,128)S(1)} %reshape_squeeze.14.ids_ref, bf16[1152,256]{1,0:T(8,128)(2,1)S(1)} %bitcast.29), custom_call_target="tpu_custom_call" | custom-call | flops 905969664 | bytes 1572864 | tf_op jit(solution)/shard_map/serve/pallas_call | solution.py:96
  30.4 0.0 copy-start.2
  30.4 0.0 all-to-all-done
  30.4 3.7 %all-to-all-start.2 = ((bf16[8,192,256]{2,1,0:T(8,128)(2,1)}), bf16[8,192,256]{2,1,0:T(8,128)(2,1)S(1)}, u32[]{:S(2)}, u32[]{:S(2)}) async-start(bf16[8,192,256]{2,1,0:T(8,128)(2,1)} %bitcast.11), calls=%async_computation.2 | async-start | bytes 1572864 | tf_op jit(solution)/shard_map/all_to_all | solution.py:257
  34.1 0.0 copy-done.2
  34.1 0.1 copy.23
  34.2 0.1 reshape.341.tasks_ref
  34.4 0.1 copy.21
  34.5 0.1 reshape.334.tasks_ref
  34.8 0.1 reshape_squeeze.15.ids_ref
  34.9 3.7 %serve.3 = bf16[1536,256]{1,0:T(8,128)(2,1)} custom-call(s32[1,1536]{1,0:T(1,128)S(1)} %reshape_squeeze.15.ids_ref, bf16[1152,256]{1,0:T(8,128)(2,1)S(1)} %bitcast.30), custom_call_target="tpu_custom_call" | custom-call | flops 905969664 | bytes 1572864 | tf_op jit(solution)/shard_map/serve/pallas_call | solution.py:96
  38.5 0.0 copy-start
  38.6 16.5 %all-to-all-done.2 = bf16[8,192,256]{2,1,0:T(8,128)(2,1)S(1)} async-done(((bf16[8,192,256]{2,1,0:T(8,128)(2,1)}), bf16[8,192,256]{2,1,0:T(8,128)(2,1)S(1)}, u32[]{:S(2)}, u32[]{:S(2)}) %all-to-all-start.2) | async-done | bytes 786464 | tf_op jit(solution)/shard_map/all_to_all | solution.py:257
  55.1 3.6 %all-to-all-start.4 = ((bf16[8,192,256]{2,1,0:T(8,128)(2,1)}), bf16[8,192,256]{2,1,0:T(8,128)(2,1)S(1)}, u32[]{:S(2)}, u32[]{:S(2)}) async-start(bf16[8,192,256]{2,1,0:T(8,128)(2,1)} %bitcast.15), calls=%async_computation.4 | async-start | bytes 1572864 | tf_op jit(solution)/shard_map/all_to_all | solution.py:257
  58.7 0.0 copy-done
  58.7 78.2 %tasks.2 = bf16[640,256]{1,0:T(8,128)(2,1)} custom-call(s32[1024]{0:T(1024)S(1)} %reshape.334.tasks_ref, s32[512]{0:T(512)S(1)} %get-tuple-element.26.slots_ref, s32[512]{0:T(512)S(1)} %get-tuple-element.24.places_ref, bf16[192,16,128]{2,1,0:T(8,128)(2,1)S(1)} %copy-done, bf16[1536,256]{1,0:T(8,128)(2,1)S(1)} %bitcast.27), custom_call_target="tpu_custom_call" | custom-call | flops 34359738368 | bytes 786432 | tf_op jit(solution)/shard_map/tasks/pallas_call | solution.py:205
  136.9 0.0 all-to-all-done.4
  136.9 3.5 %all-to-all-start.3 = ((bf16[4,160,256]{2,1,0:T(8,128)(2,1)}), bf16[4,160,256]{2,1,0:T(8,128)(2,1)S(1)}, u32[]{:S(2)}, u32[]{:S(2)}) async-start(bf16[4,160,256]{2,1,0:T(8,128)(2,1)} %bitcast.13), calls=%async_computation.3 | async-start | bytes 655360 | tf_op jit(solution)/shard_map/all_to_all | solution.py:257
  140.4 78.1 %tasks.3 = bf16[640,256]{1,0:T(8,128)(2,1)} custom-call(s32[1024]{0:T(1024)S(1)} %reshape.341.tasks_ref, s32[512]{0:T(512)S(1)} %get-tuple-element.25.slots_ref, s32[512]{0:T(512)S(1)} %get-tuple-element.23.places_ref, bf16[192,16,128]{2,1,0:T(8,128)(2,1)S(1)} %copy-done, bf16[1536,256]{1,0:T(8,128)(2,1)S(1)} %bitcast.28), custom_call_target="tpu_custom_call" | custom-call | flops 34359738368 | bytes 786432 | tf_op jit(solution)/shard_map/tasks/pallas_call | solution.py:205
  218.5 0.0 all-to-all-done.3
  218.5 3.5 %all-to-all-start.5 = ((bf16[4,160,256]{2,1,0:T(8,128)(2,1)}), bf16[4,160,256]{2,1,0:T(8,128)(2,1)S(1)}, u32[]{:S(2)}, u32[]{:S(2)}) async-start(bf16[4,160,256]{2,1,0:T(8,128)(2,1)} %bitcast.17), calls=%async_computation.5 | async-start | bytes 655360 | tf_op jit(solution)/shard_map/all_to_all | solution.py:257
  222.0 0.1 reshape.333
  222.1 0.1 reshape_squeeze.13.index_b
  222.2 0.1 reshape_squeeze.12.index_a
  222.3 6.4 %all-to-all-done.5 = bf16[4,160,256]{2,1,0:T(8,128)(2,1)S(1)} async-done(((bf16[4,160,256]{2,1,0:T(8,128)(2,1)}), bf16[4,160,256]{2,1,0:T(8,128)(2,1)S(1)}, u32[]{:S(2)}, u32[]{:S(2)}) %all-to-all-start.5) | async-done | bytes 327712 | tf_op jit(solution)/shard_map/all_to_all | solution.py:257
  228.7 2.4 %sum_blocks.1 = f32[1152,256]{1,0:T(8,128)S(1)} custom-call(s32[1,640]{1,0:T(1,128)S(1)} %reshape_squeeze.12.index_a, s32[1,640]{1,0:T(1,128)S(1)} %reshape_squeeze.13.index_b, bf16[640,256]{1,0:T(8,128)(2,1)S(1)} %bitcast.25, bf16[640,256]{1,0:T(8,128)(2,1)S(1)} %bitcast.26), custom_call_target="tpu_custom_call" | custom-call | tf_op jit(solution)/shard_map/sum_blocks/pallas_call | solution.py:245
  231.0 2.2 copy.24
  (18 shorter events, 0.4 us)
Async XLA Ops:
  2.4 24.3 %copy-start.1 = (bf16[24,48,1,256]{3,1,2,0:T(8,128)(2,1)S(1)}, bf16[24,48,1,256]{3,1,2,0:T(8,128)(2,1)}, u32[]{:S(2)}) copy-start(bf16[24,48,1,256]{3,1,2,0:T(8,128)(2,1)} %param.5) | copy-start | bytes 1769476
  9.4 13.8 %all-to-all-start.1 = ((s32[8,1,384]{2,1,0:T(1,128)}), s32[8,1,384]{2,1,0:T(1,128)S(1)}, u32[]{:S(2)}, u32[]{:S(2)}) async-start(s32[8,1,384]{2,1,0:T(1,128)} %bitcast.8), calls=%async_computation.1 | async-start | bytes 24576 | tf_op jit(solution)/shard_map/all_to_all | solution.py:257
  23.2 7.2 %all-to-all-start = ((s32[4,1,320]{2,1,0:T(1,128)}), s32[4,1,320]{2,1,0:T(1,128)S(1)}, u32[]{:S(2)}, u32[]{:S(2)}) async-start(s32[4,1,320]{2,1,0:T(1,128)} %all_to_all.32), calls=%async_computation | async-start | bytes 12288 | tf_op jit(solution)/shard_map/all_to_all | solution.py:257
  30.4 3.7 %copy-start.2 = (s32[1,1,512,4]{2,3,1,0:T(4,128)S(1)}, s32[1,1,512,4]{2,3,1,0:T(4,128)}, u32[]{:S(2)}) copy-start(s32[1,1,512,4]{2,3,1,0:T(4,128)} %param.3) | copy-start | bytes 24580
  30.4 24.7 %all-to-all-start.2 = ((bf16[8,192,256]{2,1,0:T(8,128)(2,1)}), bf16[8,192,256]{2,1,0:T(8,128)(2,1)S(1)}, u32[]{:S(2)}, u32[]{:S(2)}) async-start(bf16[8,192,256]{2,1,0:T(8,128)(2,1)} %bitcast.11), calls=%async_computation.2 | async-start | bytes 1572864 | tf_op jit(solution)/shard_map/all_to_all | solution.py:257
  38.5 20.1 %copy-start = (bf16[192,16,128]{2,1,0:T(8,128)(2,1)S(1)}, bf16[192,16,128]{2,1,0:T(8,128)(2,1)}, u32[]{:S(2)}) copy-start(bf16[192,16,128]{2,1,0:T(8,128)(2,1)} %fac_ref.3) | copy-start | bytes 2359300
  55.1 81.8 %all-to-all-start.4 = ((bf16[8,192,256]{2,1,0:T(8,128)(2,1)}), bf16[8,192,256]{2,1,0:T(8,128)(2,1)S(1)}, u32[]{:S(2)}, u32[]{:S(2)}) async-start(bf16[8,192,256]{2,1,0:T(8,128)(2,1)} %bitcast.15), calls=%async_computation.4 | async-start | bytes 1572864 | tf_op jit(solution)/shard_map/all_to_all | solution.py:257
  136.9 81.6 %all-to-all-start.3 = ((bf16[4,160,256]{2,1,0:T(8,128)(2,1)}), bf16[4,160,256]{2,1,0:T(8,128)(2,1)S(1)}, u32[]{:S(2)}, u32[]{:S(2)}) async-start(bf16[4,160,256]{2,1,0:T(8,128)(2,1)} %bitcast.13), calls=%async_computation.3 | async-start | bytes 655360 | tf_op jit(solution)/shard_map/all_to_all | solution.py:257
  218.5 10.2 %all-to-all-start.5 = ((bf16[4,160,256]{2,1,0:T(8,128)(2,1)}), bf16[4,160,256]{2,1,0:T(8,128)(2,1)S(1)}, u32[]{:S(2)}, u32[]{:S(2)}) async-start(bf16[4,160,256]{2,1,0:T(8,128)(2,1)} %bitcast.17), calls=%async_computation.5 | async-start | bytes 655360 | tf_op jit(solution)/shard_map/all_to_all | solution.py:257

commit v2 on v1

--- a/solution.py
+++ b/solution.py
@@ -123,11 +123,13 @@
 
 def task_kernel(
     tasks_ref, slots_ref, places_ref, fac_ref, got_ref, out_ref,
-    fac32, got32, dens, spread, dens_cd, partial, coulomb, routed, unroll,
+    fac32, got32, dens, spread, dens_cd, partial, coulomb, routed,
+    raw_a, raw_b, tile_a, tile_b, unroll,
 ):
     shells, funcs, terms = fac_ref.shape
     size = funcs * funcs
     count = spread.shape[1]
+    raws, tiles = (raw_a, raw_b), (tile_a, tile_b)
     fac32[...] = fac_ref[...].astype(jnp.float32)
     got32[...] = got_ref[...].astype(jnp.float32)
 
@@ -149,30 +151,51 @@
 
     lax.fori_loop(0, funcs, spread_one, 0)
 
-    def one_task(t):
+    def form(t, raw_ref, k):
         shell_i, shell_j = tasks_ref[4 * t], tasks_ref[4 * t + 1]
         shell_c, shell_d = tasks_ref[4 * t + 2], tasks_ref[4 * t + 3]
         ket = pair_rows(fac32, shell_d, fac_ref[shell_c])
         bra = pair_rows(fac32, shell_i, fac_ref[shell_j])
-        raw = dot(ket, bra, NT)
-        tile = raw * lax.rsqrt(1.0 + raw * raw)
+        raw_ref[k] = dot(ket, bra, NT).astype(raw_ref.dtype)
+
+    def bound(t, raw_ref, tile_ref, k):
         total = None
-        for f in range(funcs):
-            term = tile[f * funcs : (f + 1) * funcs] * spread[f, pl.ds(t, 1), :]
+        for f in range(0, funcs, 2):
+            terms_of = []
+            for g in (f, f + 1):
+                rows = slice(g * funcs, (g + 1) * funcs)
+                raw = raw_ref[k, rows, :]
+                tile = raw * lax.rsqrt(raw * raw + jnp.ones_like(raw))
+                tile_ref[k, rows, :] = tile
+                held = jnp.broadcast_to(spread[g, pl.ds(t, 1), :], (funcs, size))
+                terms_of.append(tile * held.astype(tile.dtype))
+            term = (terms_of[0] + terms_of[1]).astype(jnp.float32)
             total = term if total is None else total + term
         place = pl.ds(pl.multiple_of(t * funcs, funcs), funcs)
         for lane in range(size // 128):
             partial[lane, place, :] = total[:, lane * 128 : (lane + 1) * 128]
+
+    def contract(t, tile_ref, k):
         weights = jnp.broadcast_to(dens_cd[pl.ds(t, 1), :], (16, size)).astype(jnp.bfloat16)
-        summed = dot(weights, tile.astype(jnp.bfloat16), NN)
+        summed = dot(weights, tile_ref[k], NN)
         coulomb[pl.ds(t, 1), :] = summed[0:1]
 
-    def some_tasks(step, carry):
-        for k in range(unroll):
-            one_task(step * unroll + k)
-        return carry
-
-    lax.fori_loop(0, count // unroll, some_tasks, 0)
+    batches = count // unroll
+
+    def first_of(batch):
+        return jnp.clip(batch, 0, batches - 1) * unroll
+
+    def steps(pair, carry):
+        for odd in range(2):
+            batch = 2 * pair + odd
+            here, there = (0, 1) if odd == 0 else (1, 0)
+            for k in range(unroll):
+                contract(first_of(batch - 2) + k, tiles[here], k)
+                bound(first_of(batch - 1) + k, raws[there], tiles[there], k)
+                form(first_of(batch) + k, raws[here], k)
+        return carry
+
+    lax.fori_loop(0, (batches + 2) // 2, steps, 0)
 
     dens[0] = coulomb[...] * tile_scale
     dens[1] = jnp.zeros((count, size), jnp.float32)
@@ -216,7 +239,8 @@
             pltpu.VMEM((size // 128, count * funcs, 128), f32),
             pltpu.VMEM((count, size), f32),
             pltpu.VMEM((out_rows, size), f32),
-        ],
+        ]
+        + [pltpu.VMEM((unroll, size, size), jnp.bfloat16)] * 4,
         compiler_params=PARAMS,
         cost_estimate=pl.CostEstimate(
             flops=16 * count * size * size * terms,
@@ -276,15 +300,17 @@
     target = jnp.stack([shell_j, shell_c], axis=1).reshape(-1)
     position = jnp.repeat(shell_i % rows_per_device, 2) * cols_dev + target // ket_count
     ket_bucket = target % ket_count * 2 + half_of
-    slots, asked = plan(
-        [bra_bucket[None], ket_bucket[None]],
-        [wanted[None], position[None]],
-        ((2 * bra_count, cap_bra), (2 * ket_count, cap_ket)),
+    slot_bra, asked_bra = plan(
+        [bra_bucket[None]], [wanted[None]], ((2 * bra_count, cap_bra),)
     )
-    asked_bra = trade(asked[0].reshape(bra_count, 2 * cap_bra), "bra")
+    asked_bra = trade(asked_bra[0].reshape(bra_count, 2 * cap_bra), "bra")
     asked_bra = asked_bra.reshape(bra_count, 2, cap_bra).transpose(1, 0, 2)
-    arrived = trade(asked[1].reshape(ket_count, 2 * cap_ket), "ket")
-    arrived = arrived.reshape(ket_count, 2, cap_ket).transpose(1, 0, 2)
+    served = [serve(asked_bra[which].reshape(1, -1), table) for which in range(2)]
+    late_bucket, served[0] = lax.optimization_barrier((ket_bucket, served[0]))
+    slot_ket, asked_ket = plan(
+        [late_bucket[None]], [position[None]], ((2 * ket_count, cap_ket),)
+    )
+    slots = (slot_bra[0], slot_ket[0])
 
     def per_half(slot, capacity, which):
         bucket, place = slot // capacity, slot % capacity
@@ -293,8 +319,7 @@
 
     results = []
     for which in range(2):
-        served = serve(asked_bra[which].reshape(1, -1), table)
-        got = trade(served.reshape(bra_count, cap_bra, size), "bra")
+        got = trade(served[which].reshape(bra_count, cap_bra, size), "bra")
         outgoing = run_tasks(
             quartets[which * half : (which + 1) * half].reshape(-1),
             per_half(slots[0].reshape(-1), cap_bra, which),
@@ -304,6 +329,10 @@
             ket_count * cap_ket,
             4,
         )
+        if which == 0:
+            sent, outgoing = lax.optimization_barrier((asked_ket[0], outgoing))
+            arrived = trade(sent.reshape(ket_count, 2 * cap_ket), "ket")
+            arrived = arrived.reshape(ket_count, 2, cap_ket).transpose(1, 0, 2)
         back = trade(outgoing.reshape(ket_count, cap_ket, size), "ket")
         results.append(back.reshape(-1, size))
     fock = sum_blocks(

time: 234 us -> 155 us (0.66)
  Pallas kernels: 172 us -> 93.5 us
    pallas_call x2, Pallas kernels: 156 us -> 77.9 us  [run_tasks(): pl.pallas_call(functools.partial(task_kernel, unroll=unroll), out_shape=j...]
    pallas_call x1 -> x2, Pallas kernels: 5.6 us -> 5.83 us  [plan(): pl.pallas_call(kernel, out_shape=[jax.ShapeDtypeStruct((1, items), jnp.in...]
  transfers between devices with their start and end apart: 6 -> 6, of which waited for: 3 -> 4; matrix products, arithmetic and copies ran while one was open for 1% -> 1% of each run, Pallas kernels for 70% -> 54%
where the time goes in v2:
time: 155 us; the launch traced here: 154 us
  Pallas kernels  93.5 us (60%)
  waiting for transfers between devices  28.7 us (19%)
  starting transfers between devices  24.5 us (16%)
  local copies, waits for them, and re-layouts  6.15 us (4%)
    pallas_call x2, Pallas kernels, run_tasks(): pl.pallas_call(functools.partial(task_kernel, unroll=unroll), out_shape=j...  77.9 us
    all_to_all x6, waiting for transfers between devices, trade(): return lax.all_to_all(array, axis, split_axis=0, concat_axis=0, tiled=True)  28.7 us
    all_to_all x6, starting transfers between devices, trade(): return lax.all_to_all(array, axis, split_axis=0, concat_axis=0, tiled=True)  24.5 us
    pallas_call x2, Pallas kernels, serve(): pl.pallas_call(serve_kernel, grid=(total // wide,), out_shape=jax.ShapeDt...  7.38 us
    pallas_call x2, Pallas kernels, plan(): pl.pallas_call(kernel, out_shape=[jax.ShapeDtypeStruct((1, items), jnp.in...  5.83 us
  transfers between devices with their start and end apart: 6, of which 4 were waited for; matrix products, arithmetic and copies ran while one was open for 1% of the time, Pallas kernels for 54%

profile of v2, /device:TPU:0, one launch (start us, length us, event | category | flops | bytes accessed | tf_op | source)
XLA Modules:
  0.0 154.3 jit_solution(9118046358552859488)
XLA Ops:
  0.0 0.0 copy-start.2
  0.0 0.9 slice_remainder_fusion
  1.0 0.2 copy.18
  1.2 0.2 ne.199
  1.3 0.0 copy-start.1
  1.4 0.1 copy.19
  1.5 0.2 rem.181
  1.7 0.1 broadcast_in_dim.12
  1.8 0.2 reshape.295
  2.0 0.1 copy.20
  2.2 0.2 div.87
  2.4 4.2 %plan.2 = (s32[1,1024]{1,0:T(1,128)S(1)}, s32[1,3072]{1,0:T(1,128)}) custom-call(s32[1,1024]{1,0:T(1,128)S(1)} %get-tuple-element.40.refs_0_, s32[1,1024]{1,0:T(1,128)S(1)} %get-tuple-element.39.refs_1_), custom_call_target="tpu_custom_call" | custom-call | tf_op jit(solution)/shard_map/plan/pallas_call | solution.py:72
  6.6 7.3 %all-to-all-start = ((s32[8,1,384]{2,1,0:T(1,128)}), s32[8,1,384]{2,1,0:T(1,128)S(1)}, u32[]{:S(2)}, u32[]{:S(2)}) async-start(s32[8,1,384]{2,1,0:T(1,128)} %bitcast.2), calls=%async_computation | async-start | bytes 24576 | tf_op jit(solution)/shard_map/all_to_all | solution.py:281
  13.8 0.0 copy-done.2
  13.9 0.1 copy.17
  14.0 0.2 reshape.294
  14.2 6.1 %all-to-all-done = s32[8,1,384]{2,1,0:T(1,128)S(1)} async-done(((s32[8,1,384]{2,1,0:T(1,128)}), s32[8,1,384]{2,1,0:T(1,128)S(1)}, u32[]{:S(2)}, u32[]{:S(2)}) %all-to-all-start) | async-done | bytes 12320 | tf_op jit(solution)/shard_map/all_to_all | solution.py:281
  20.4 0.1 reshape.296
  20.5 0.1 reshape_squeeze.12.ids_ref
  20.6 0.0 copy-done.1
  20.6 3.7 %serve.2 = bf16[1536,256]{1,0:T(8,128)(2,1)} custom-call(s32[1,1536]{1,0:T(1,128)S(1)} %reshape_squeeze.12.ids_ref, bf16[1152,256]{1,0:T(8,128)(2,1)S(1)} %bitcast.31), custom_call_target="tpu_custom_call" | custom-call | flops 905969664 | bytes 1572864 | tf_op jit(solution)/shard_map/serve/pallas_call | solution.py:96
  24.3 3.5 %all-to-all-start.1 = ((bf16[8,192,256]{2,1,0:T(8,128)(2,1)}), bf16[8,192,256]{2,1,0:T(8,128)(2,1)S(1)}, u32[]{:S(2)}, u32[]{:S(2)}) async-start(bf16[8,192,256]{2,1,0:T(8,128)(2,1)} %bitcast.11), calls=%async_computation.1 | async-start | bytes 1572864 | tf_op jit(solution)/shard_map/all_to_all | solution.py:281
  27.9 0.2 reshape.298
  28.1 0.1 copy.23
  28.2 0.1 reshape.299.tasks_ref
  28.3 0.1 broadcast_in_dim.14
  28.5 0.2 mul.49
  28.7 0.1 reshape_squeeze.15.ids_ref
  28.8 1.7 %plan.3 = (s32[1,1024]{1,0:T(1,128)S(1)}, s32[1,1280]{1,0:T(1,128)S(1)}) custom-call(s32[1,1024]{1,0:T(1,128)S(1)} %bitcast.30, s32[1,1024]{1,0:T(1,128)S(1)} %fusion.14.refs_1_), custom_call_target="tpu_custom_call" | custom-call | tf_op jit(solution)/shard_map/plan/pallas_call | solution.py:72
  30.5 3.7 %serve.3 = bf16[1536,256]{1,0:T(8,128)(2,1)} custom-call(s32[1,1536]{1,0:T(1,128)S(1)} %reshape_squeeze.15.ids_ref, bf16[1152,256]{1,0:T(8,128)(2,1)S(1)} %bitcast.32), custom_call_target="tpu_custom_call" | custom-call | flops 905969664 | bytes 1572864 | tf_op jit(solution)/shard_map/serve/pallas_call | solution.py:96
  34.2 0.0 copy-start
  34.3 12.6 %all-to-all-done.1 = bf16[8,192,256]{2,1,0:T(8,128)(2,1)S(1)} async-done(((bf16[8,192,256]{2,1,0:T(8,128)(2,1)}), bf16[8,192,256]{2,1,0:T(8,128)(2,1)S(1)}, u32[]{:S(2)}, u32[]{:S(2)}) %all-to-all-start.1) | async-done | bytes 786464 | tf_op jit(solution)/shard_map/all_to_all | solution.py:281
  46.9 3.5 %all-to-all-start.4 = ((bf16[8,192,256]{2,1,0:T(8,128)(2,1)}), bf16[8,192,256]{2,1,0:T(8,128)(2,1)S(1)}, u32[]{:S(2)}, u32[]{:S(2)}) async-start(bf16[8,192,256]{2,1,0:T(8,128)(2,1)} %bitcast.16), calls=%async_computation.4 | async-start | bytes 1572864 | tf_op jit(solution)/shard_map/all_to_all | solution.py:281
  50.4 0.0 copy-done
  50.5 38.9 %tasks.2 = bf16[640,256]{1,0:T(8,128)(2,1)} custom-call(s32[1024]{0:T(1024)S(1)} %reshape.299.tasks_ref, s32[512]{0:T(512)S(1)} %get-tuple-element.43.slots_ref, s32[512]{0:T(512)S(1)} %get-tuple-element.32.places_ref, bf16[192,16,128]{2,1,0:T(8,128)(2,1)S(1)} %copy-done, bf16[1536,256]{1,0:T(8,128)(2,1)S(1)} %bitcast.28), custom_call_target="tpu_custom_call" | custom-call | flops 34359738368 | bytes 786432 | tf_op jit(solution)/shard_map/tasks/pallas_call | solution.py:228
  89.4 0.7 all_to_all.32
  90.1 0.0 all-to-all-done.4
  90.1 3.2 %all-to-all-start.2 = ((s32[4,1,320]{2,1,0:T(1,128)}), s32[4,1,320]{2,1,0:T(1,128)S(1)}, u32[]{:S(2)}, u32[]{:S(2)}) async-start(s32[4,1,320]{2,1,0:T(1,128)} %all_to_all.32), calls=%async_computation.2 | async-start | bytes 12288 | tf_op jit(solution)/shard_map/all_to_all | solution.py:281
  93.3 0.1 copy.25
  93.5 0.1 reshape.305.tasks_ref
  93.6 3.5 %all-to-all-done.2 = s32[4,1,320]{2,1,0:T(1,128)S(1)} async-done(((s32[4,1,320]{2,1,0:T(1,128)}), s32[4,1,320]{2,1,0:T(1,128)S(1)}, u32[]{:S(2)}, u32[]{:S(2)}) %all-to-all-start.2) | async-done | bytes 5152 | tf_op jit(solution)/shard_map/all_to_all | solution.py:281
  97.1 3.5 %all-to-all-start.3 = ((bf16[4,160,256]{2,1,0:T(8,128)(2,1)}), bf16[4,160,256]{2,1,0:T(8,128)(2,1)S(1)}, u32[]{:S(2)}, u32[]{:S(2)}) async-start(bf16[4,160,256]{2,1,0:T(8,128)(2,1)} %bitcast.14), calls=%async_computation.3 | async-start | bytes 655360 | tf_op jit(solution)/shard_map/all_to_all | solution.py:281
  100.6 39.0 %tasks.3 = bf16[640,256]{1,0:T(8,128)(2,1)} custom-call(s32[1024]{0:T(1024)S(1)} %reshape.305.tasks_ref, s32[512]{0:T(512)S(1)} %get-tuple-element.44.slots_ref, s32[512]{0:T(512)S(1)} %get-tuple-element.31.places_ref, bf16[192,16,128]{2,1,0:T(8,128)(2,1)S(1)} %copy-done, bf16[1536,256]{1,0:T(8,128)(2,1)S(1)} %bitcast.29), custom_call_target="tpu_custom_call" | custom-call | flops 34359738368 | bytes 786432 | tf_op jit(solution)/shard_map/tasks/pallas_call | solution.py:228
  139.5 0.0 all-to-all-done.3
  139.5 3.5 %all-to-all-start.5 = ((bf16[4,160,256]{2,1,0:T(8,128)(2,1)}), bf16[4,160,256]{2,1,0:T(8,128)(2,1)S(1)}, u32[]{:S(2)}, u32[]{:S(2)}) async-start(bf16[4,160,256]{2,1,0:T(8,128)(2,1)} %bitcast.18), calls=%async_computation.5 | async-start | bytes 655360 | tf_op jit(solution)/shard_map/all_to_all | solution.py:281
  143.0 0.1 reshape.302
  143.1 0.1 reshape_squeeze.14.index_b
  143.2 0.1 reshape_squeeze.13.index_a
  143.3 6.4 %all-to-all-done.5 = bf16[4,160,256]{2,1,0:T(8,128)(2,1)S(1)} async-done(((bf16[4,160,256]{2,1,0:T(8,128)(2,1)}), bf16[4,160,256]{2,1,0:T(8,128)(2,1)S(1)}, u32[]{:S(2)}, u32[]{:S(2)}) %all-to-all-start.5) | async-done | bytes 327712 | tf_op jit(solution)/shard_map/all_to_all | solution.py:281
  149.8 2.4 %sum_blocks.1 = f32[1152,256]{1,0:T(8,128)S(1)} custom-call(s32[1,640]{1,0:T(1,128)S(1)} %reshape_squeeze.13.index_a, s32[1,640]{1,0:T(1,128)S(1)} %reshape_squeeze.14.index_b, bf16[640,256]{1,0:T(8,128)(2,1)S(1)} %bitcast.26, bf16[640,256]{1,0:T(8,128)(2,1)S(1)} %bitcast.27), custom_call_target="tpu_custom_call" | custom-call | tf_op jit(solution)/shard_map/sum_blocks/pallas_call | solution.py:269
  152.1 2.2 %copy.26 = f32[24,48,1,256]{3,2,1,0:T(1,128)} copy(f32[24,48,1,256]{3,1,0,2:T(8,128)S(1)} %bitcast.25) | data formatting | bytes 2359296 | tf_op jit(solution)/shard_map/reshape | solution.py:343
  (21 shorter events, 0.4 us)
Async XLA Ops:
  0.0 13.8 %copy-start.2 = (s32[1,1,512,4]{2,3,1,0:T(4,128)S(1)}, s32[1,1,512,4]{2,3,1,0:T(4,128)}, u32[]{:S(2)}) copy-start(s32[1,1,512,4]{2,3,1,0:T(4,128)} %param.3) | copy-start | bytes 24580
  1.3 19.3 %copy-start.1 = (bf16[24,48,1,256]{3,1,2,0:T(8,128)(2,1)S(1)}, bf16[24,48,1,256]{3,1,2,0:T(8,128)(2,1)}, u32[]{:S(2)}) copy-start(bf16[24,48,1,256]{3,1,2,0:T(8,128)(2,1)} %param.5) | copy-start | bytes 1769476
  6.6 13.8 %all-to-all-start = ((s32[8,1,384]{2,1,0:T(1,128)}), s32[8,1,384]{2,1,0:T(1,128)S(1)}, u32[]{:S(2)}, u32[]{:S(2)}) async-start(s32[8,1,384]{2,1,0:T(1,128)} %bitcast.2), calls=%async_computation | async-start | bytes 24576 | tf_op jit(solution)/shard_map/all_to_all | solution.py:281
  24.3 22.6 %all-to-all-start.1 = ((bf16[8,192,256]{2,1,0:T(8,128)(2,1)}), bf16[8,192,256]{2,1,0:T(8,128)(2,1)S(1)}, u32[]{:S(2)}, u32[]{:S(2)}) async-start(bf16[8,192,256]{2,1,0:T(8,128)(2,1)} %bitcast.11), calls=%async_computation.1 | async-start | bytes 1572864 | tf_op jit(solution)/shard_map/all_to_all | solution.py:281
  34.2 16.3 %copy-start = (bf16[192,16,128]{2,1,0:T(8,128)(2,1)S(1)}, bf16[192,16,128]{2,1,0:T(8,128)(2,1)}, u32[]{:S(2)}) copy-start(bf16[192,16,128]{2,1,0:T(8,128)(2,1)} %fac_ref.3) | copy-start | bytes 2359300
  46.9 43.2 %all-to-all-start.4 = ((bf16[8,192,256]{2,1,0:T(8,128)(2,1)}), bf16[8,192,256]{2,1,0:T(8,128)(2,1)S(1)}, u32[]{:S(2)}, u32[]{:S(2)}) async-start(bf16[8,192,256]{2,1,0:T(8,128)(2,1)} %bitcast.16), calls=%async_computation.4 | async-start | bytes 1572864 | tf_op jit(solution)/shard_map/all_to_all | solution.py:281
  90.1 7.0 %all-to-all-start.2 = ((s32[4,1,320]{2,1,0:T(1,128)}), s32[4,1,320]{2,1,0:T(1,128)S(1)}, u32[]{:S(2)}, u32[]{:S(2)}) async-start(s32[4,1,320]{2,1,0:T(1,128)} %all_to_all.32), calls=%async_computation.2 | async-start | bytes 12288 | tf_op jit(solution)/shard_map/all_to_all | solution.py:281
  97.1 42.4 %all-to-all-start.3 = ((bf16[4,160,256]{2,1,0:T(8,128)(2,1)}), bf16[4,160,256]{2,1,0:T(8,128)(2,1)S(1)}, u32[]{:S(2)}, u32[]{:S(2)}) async-start(bf16[4,160,256]{2,1,0:T(8,128)(2,1)} %bitcast.14), calls=%async_computation.3 | async-start | bytes 655360 | tf_op jit(solution)/shard_map/all_to_all | solution.py:281
  139.5 10.2 %all-to-all-start.5 = ((bf16[4,160,256]{2,1,0:T(8,128)(2,1)}), bf16[4,160,256]{2,1,0:T(8,128)(2,1)S(1)}, u32[]{:S(2)}, u32[]{:S(2)}) async-start(bf16[4,160,256]{2,1,0:T(8,128)(2,1)} %bitcast.18), calls=%async_computation.5 | async-start | bytes 655360 | tf_op jit(solution)/shard_map/all_to_all | solution.py:281

commit v3 on v2

--- a/solution.py
+++ b/solution.py
@@ -10,6 +10,7 @@
 tile_scale = 0.0625
 NT = (((1,), (1,)), ((), ()))
 NN = (((1,), (0,)), ((), ()))
+id_rows = 16
 VMEM = pl.BlockSpec(memory_space=pltpu.VMEM)
 SMEM = pl.BlockSpec(memory_space=pltpu.SMEM)
 PARAMS = pltpu.CompilerParams(vmem_limit_bytes=48 * 1024 * 1024)
@@ -122,7 +123,7 @@
 
 
 def task_kernel(
-    tasks_ref, slots_ref, places_ref, fac_ref, got_ref, out_ref,
+    tasks_ref, slots_ref, places_ref, fac_ref, got_ref, ids_ref, out_ref,
     fac32, got32, dens, spread, dens_cd, partial, coulomb, routed,
     raw_a, raw_b, tile_a, tile_b, unroll,
 ):
@@ -149,7 +150,7 @@
         spread[f] = dot(dens_jd, hot((row_hi == col_lo) & (row_lo == f)), NN)
         return carry
 
-    lax.fori_loop(0, funcs, spread_one, 0)
+    lax.fori_loop(0, funcs, spread_one, 0, unroll=4)
 
     def form(t, raw_ref, k):
         shell_i, shell_j = tasks_ref[4 * t], tasks_ref[4 * t + 1]
@@ -207,9 +208,14 @@
         dens[1] += dot(rows, hot((row_hi == col_hi) & (col_lo == e)), NN)
         return carry
 
-    lax.fori_loop(0, funcs, fold, 0)
+    lax.fori_loop(0, funcs, fold, 0, unroll=4)
     dens[1] = dens[1] * (-0.5 * tile_scale)
     routed[...] = jnp.zeros_like(routed)
+    owners = ids_ref.shape[0] // 2
+    stride = routed.shape[0] // owners
+    for owner in range(owners):
+        last = (owner + 1) * stride - id_rows
+        routed[last : last + 2, :] = ids_ref[2 * owner : 2 * owner + 2, :]
 
     def route(t, carry):
         for side in range(2):
@@ -220,7 +226,7 @@
     out_ref[...] = routed[...].astype(jnp.bfloat16)
 
 
-def run_tasks(tasks, slots, places, factors, got, out_rows, unroll):
+def run_tasks(tasks, slots, places, factors, got, ids, out_rows, unroll):
     count = tasks.shape[0] // 4
     shells, funcs, terms = factors.shape
     size = funcs * funcs
@@ -228,7 +234,7 @@
     return pl.pallas_call(
         functools.partial(task_kernel, unroll=unroll),
         out_shape=jax.ShapeDtypeStruct((out_rows, size), jnp.bfloat16),
-        in_specs=[SMEM, SMEM, SMEM, VMEM, VMEM],
+        in_specs=[SMEM, SMEM, SMEM, VMEM, VMEM, VMEM],
         out_specs=VMEM,
         scratch_shapes=[
             pltpu.VMEM((shells, funcs, terms), f32),
@@ -248,33 +254,38 @@
             transcendentals=count * size * size,
         ),
         name="tasks",
-    )(tasks, slots, places, factors, got)
-
-
-def sum_kernel(index_a, index_b, block_a, block_b, out_ref):
+    )(tasks, slots, places, factors, got, ids)
+
+
+def sum_kernel(block_a, block_b, out_ref, *, sources):
     rows = out_ref.shape[0]
+    stride = block_a.shape[0] // sources
     first = pl.program_id(0) * rows
+    here = (iota((rows, stride), 0) + first).astype(jnp.float32)
     total = None
-    for index, block in ((index_a, block_a), (index_b, block_b)):
-        picked = hot(index[...] == iota((rows, index.shape[1]), 0) + first)
-        term = dot(picked, block[...], NN)
-        total = term if total is None else total + term
+    for block in (block_a, block_b):
+        for source in range(sources):
+            held = block[source * stride : (source + 1) * stride, :]
+            ids = held[stride - id_rows :, :].astype(jnp.float32)
+            index = (ids[0:1] * 64.0 + ids[1:2])[:, :stride]
+            term = dot(hot(jnp.broadcast_to(index, here.shape) == here), held, NN)
+            total = term if total is None else total + term
     out_ref[...] = total
 
 
-def sum_blocks(indices, blocks, total):
+def sum_blocks(blocks, sources, total):
     rows = 128
     size = blocks[0].shape[1]
     whole = lambda array: pl.BlockSpec(array.shape, lambda k: (0, 0))
     return pl.pallas_call(
-        sum_kernel,
+        functools.partial(sum_kernel, sources=sources),
         grid=(total // rows,),
         out_shape=jax.ShapeDtypeStruct((total, size), jnp.float32),
-        in_specs=[whole(indices[0]), whole(indices[1]), whole(blocks[0]), whole(blocks[1])],
+        in_specs=[whole(blocks[0]), whole(blocks[1])],
         out_specs=pl.BlockSpec((rows, size), lambda k: (k, 0)),
         compiler_params=PARAMS,
         name="sum_blocks",
-    )(*indices, *blocks)
+    )(*blocks)
 
 
 def trade(array, axis):
@@ -312,34 +323,32 @@
     )
     slots = (slot_bra[0], slot_ket[0])
 
-    def per_half(slot, capacity, which):
+    def per_half(slot, capacity, stride, which):
         bucket, place = slot // capacity, slot % capacity
-        local = bucket // 2 * capacity + place
+        local = bucket // 2 * stride + place
         return local[which * task_count : (which + 1) * task_count]
+
+    stride = cap_ket + id_rows
+    ids = asked_ket[0].reshape(ket_count, 2, cap_ket)
+    ids = jnp.stack([ids >> 6, ids & 63], axis=2).astype(jnp.float32)
+    ids = jnp.pad(ids, ((0, 0), (0, 0), (0, 0), (0, size - cap_ket)), constant_values=-1.0)
 
     results = []
     for which in range(2):
         got = trade(served[which].reshape(bra_count, cap_bra, size), "bra")
         outgoing = run_tasks(
             quartets[which * half : (which + 1) * half].reshape(-1),
-            per_half(slots[0].reshape(-1), cap_bra, which),
-            per_half(slots[1].reshape(-1), cap_ket, which),
+            per_half(slots[0].reshape(-1), cap_bra, cap_bra, which),
+            per_half(slots[1].reshape(-1), cap_ket, stride, which),
             factors,
             got.reshape(-1, size),
-            ket_count * cap_ket,
+            ids[:, which].reshape(-1, size),
+            ket_count * stride,
             4,
         )
-        if which == 0:
-            sent, outgoing = lax.optimization_barrier((asked_ket[0], outgoing))
-            arrived = trade(sent.reshape(ket_count, 2 * cap_ket), "ket")
-            arrived = arrived.reshape(ket_count, 2, cap_ket).transpose(1, 0, 2)
-        back = trade(outgoing.reshape(ket_count, cap_ket, size), "ket")
+        back = trade(outgoing.reshape(ket_count, stride, size), "ket")
         results.append(back.reshape(-1, size))
-    fock = sum_blocks(
-        [arrived[0].reshape(1, -1), arrived[1].reshape(1, -1)],
-        results,
-        rows_per_device * cols_dev,
-    )
+    fock = sum_blocks(results, ket_count, rows_per_device * cols_dev)
     return fock.reshape(rows_per_device, cols_dev, 1, size)
 
 

time: 155 us -> 138 us (0.89)
  waiting for transfers between devices: 28.7 us -> 18.2 us
  blocking collectives: 0 us -> 10.1 us
  Pallas kernels: 93.5 us -> 84.7 us
  starting transfers between devices: 24.5 us -> 17.8 us
    all_to_all x6 -> x4, waiting for transfers between devices: 28.7 us -> 18.2 us  [trade(): return lax.all_to_all(array, axis, split_axis=0, concat_axis=0, tiled=True)]
    all_to_all x0 -> x1, blocking collectives: none -> 10.1 us  [trade(): return lax.all_to_all(array, axis, split_axis=0, concat_axis=0, tiled=True)]
    pallas_call x2, Pallas kernels: 77.9 us -> 68.8 us  [run_tasks(): pl.pallas_call(functools.partial(task_kernel, unroll=unroll), out_shape=j...]
    all_to_all x6 -> x4, starting transfers between devices: 24.5 us -> 17.8 us  [trade(): return lax.all_to_all(array, axis, split_axis=0, concat_axis=0, tiled=True)]
  transfers between devices with their start and end apart: 6 -> 4, of which waited for: 4 -> 2; matrix products, arithmetic and copies ran while one was open for 1% -> 1% of each run, Pallas kernels for 54% -> 54%
where the time goes in v3:
time: 138 us
  Pallas kernels  84.7 us (61%)
  waiting for transfers between devices  18.2 us (13%)
  starting transfers between devices  17.8 us (13%)
  blocking collectives  10.1 us (7%)
  local copies, waits for them, and re-layouts  5.4 us (4%)
    pallas_call x2, Pallas kernels, run_tasks(): pl.pallas_call(functools.partial(task_kernel, unroll=unroll), out_shape=j...  68.8 us
    all_to_all x4, waiting for transfers between devices, trade(): return lax.all_to_all(array, axis, split_axis=0, concat_axis=0, tiled=True)  18.2 us
    all_to_all x4, starting transfers between devices, trade(): return lax.all_to_all(array, axis, split_axis=0, concat_axis=0, tiled=True)  17.8 us
    all_to_all x1, blocking collectives, trade(): return lax.all_to_all(array, axis, split_axis=0, concat_axis=0, tiled=True)  10.1 us
    pallas_call x2, Pallas kernels, serve(): pl.pallas_call(serve_kernel, grid=(total // wide,), out_shape=jax.ShapeDt...  7.37 us
    pallas_call x2, Pallas kernels, plan(): pl.pallas_call(kernel, out_shape=[jax.ShapeDtypeStruct((1, items), jnp.in...  5.83 us
  transfers between devices with their start and end apart: 4, of which 2 were waited for; matrix products, arithmetic and copies ran while one was open for 1% of the time, Pallas kernels for 54%

profile of v3, /device:TPU:0, one launch (start us, length us, event | category | flops | bytes accessed | tf_op | source)
XLA Modules:
  0.0 137.8 jit_solution(87655360203413747)
XLA Ops:
  0.0 0.0 copy-start.2
  0.0 0.9 slice_remainder_fusion
  1.0 0.2 copy.22
  1.2 0.2 ne.199
  1.3 0.1 copy.23
  1.5 0.2 rem.171
  1.7 0.1 broadcast_in_dim.12
  1.8 0.2 reshape.312
  2.0 0.1 copy.24
  2.2 0.0 copy-start.1
  2.2 0.2 div.85
  2.4 4.2 %plan.2 = (s32[1,1024]{1,0:T(1,128)S(1)}, s32[1,3072]{1,0:T(1,128)}) custom-call(s32[1,1024]{1,0:T(1,128)S(1)} %get-tuple-element.38.refs_0_, s32[1,1024]{1,0:T(1,128)S(1)} %get-tuple-element.37.refs_1_), custom_call_target="tpu_custom_call" | custom-call | tf_op jit(solution)/shard_map/plan/pallas_call | solution.py:73
  6.5 7.3 %all-to-all-start = ((s32[8,1,384]{2,1,0:T(1,128)}), s32[8,1,384]{2,1,0:T(1,128)S(1)}, u32[]{:S(2)}, u32[]{:S(2)}) async-start(s32[8,1,384]{2,1,0:T(1,128)} %bitcast.4), calls=%async_computation | async-start | bytes 24576 | tf_op jit(solution)/shard_map/all_to_all | solution.py:292
  13.8 0.0 copy-done.2
  13.9 0.1 copy.25
  14.1 0.2 reshape.313
  14.3 0.2 reshape.316
  14.5 0.1 copy.30
  14.6 0.1 reshape.321.tasks_ref
  14.7 0.1 copy.21
  14.9 0.1 reshape.310.tasks_ref
  15.0 0.1 broadcast_in_dim.14
  15.1 0.2 mul.50
  15.3 5.1 %all-to-all-done = s32[8,1,384]{2,1,0:T(1,128)S(1)} async-done(((s32[8,1,384]{2,1,0:T(1,128)}), s32[8,1,384]{2,1,0:T(1,128)S(1)}, u32[]{:S(2)}, u32[]{:S(2)}) %all-to-all-start) | async-done | bytes 12320 | tf_op jit(solution)/shard_map/all_to_all | solution.py:292
  20.4 0.1 reshape.314
  20.5 0.1 reshape_squeeze.12.ids_ref
  20.6 0.0 copy-done.1
  20.6 3.7 %serve.2 = bf16[1536,256]{1,0:T(8,128)(2,1)} custom-call(s32[1,1536]{1,0:T(1,128)S(1)} %reshape_squeeze.12.ids_ref, bf16[1152,256]{1,0:T(8,128)(2,1)S(1)} %bitcast.35), custom_call_target="tpu_custom_call" | custom-call | flops 905969664 | bytes 1572864 | tf_op jit(solution)/shard_map/serve/pallas_call | solution.py:97
  24.3 3.5 %all-to-all-start.1 = ((bf16[8,192,256]{2,1,0:T(8,128)(2,1)}), bf16[8,192,256]{2,1,0:T(8,128)(2,1)S(1)}, u32[]{:S(2)}, u32[]{:S(2)}) async-start(bf16[8,192,256]{2,1,0:T(8,128)(2,1)} %bitcast.11), calls=%async_computation.1 | async-start | bytes 1572864 | tf_op jit(solution)/shard_map/all_to_all | solution.py:292
  27.9 0.1 reshape_squeeze.14.ids_ref
  28.0 1.7 %plan.3 = (s32[1,1024]{1,0:T(1,128)S(1)}, s32[1,1280]{1,0:T(1,128)S(1)}) custom-call(s32[1,1024]{1,0:T(1,128)S(1)} %bitcast.34, s32[1,1024]{1,0:T(1,128)S(1)} %fusion.14.refs_1_), custom_call_target="tpu_custom_call" | custom-call | tf_op jit(solution)/shard_map/plan/pallas_call | solution.py:73
  29.7 0.1 shift_right_arithmetic.18
  29.8 0.1 and.131
  30.0 3.7 %serve.3 = bf16[1536,256]{1,0:T(8,128)(2,1)} custom-call(s32[1,1536]{1,0:T(1,128)S(1)} %reshape_squeeze.14.ids_ref, bf16[1152,256]{1,0:T(8,128)(2,1)S(1)} %bitcast.36), custom_call_target="tpu_custom_call" | custom-call | flops 905969664 | bytes 1572864 | tf_op jit(solution)/shard_map/serve/pallas_call | solution.py:97
  33.7 0.0 copy-start
  33.8 13.1 %all-to-all-done.1 = bf16[8,192,256]{2,1,0:T(8,128)(2,1)S(1)} async-done(((bf16[8,192,256]{2,1,0:T(8,128)(2,1)}), bf16[8,192,256]{2,1,0:T(8,128)(2,1)S(1)}, u32[]{:S(2)}, u32[]{:S(2)}) %all-to-all-start.1) | async-done | bytes 786464 | tf_op jit(solution)/shard_map/all_to_all | solution.py:292
  46.9 3.5 %all-to-all-start.3 = ((bf16[8,192,256]{2,1,0:T(8,128)(2,1)}), bf16[8,192,256]{2,1,0:T(8,128)(2,1)S(1)}, u32[]{:S(2)}, u32[]{:S(2)}) async-start(bf16[8,192,256]{2,1,0:T(8,128)(2,1)} %bitcast.15), calls=%async_computation.3 | async-start | bytes 1572864 | tf_op jit(solution)/shard_map/all_to_all | solution.py:292
  50.4 0.0 copy-done
  50.4 34.8 %tasks.2 = bf16[704,256]{1,0:T(8,128)(2,1)} custom-call(s32[1024]{0:T(1024)S(1)} %reshape.310.tasks_ref, s32[512]{0:T(512)S(1)} %get-tuple-element.41.slots_ref, s32[512]{0:T(512)S(1)} %get-tuple-element.30.places_ref, bf16[192,16,128]{2,1,0:T(8,128)(2,1)S(1)} %copy-done, bf16[1536,256]{1,0:T(8,128)(2,1)S(1)} %bitcast.31, f32[8,256]{1,0:T(8,128)S(1)} %reshape_squeeze.13.ids_ref), custom_call_target="tpu_custom_call" | custom-call | flops 34359738368 | bytes 786432 | tf_op jit(solution)/shard_map/tasks/pallas_call | solution.py:234
  85.2 0.0 all-to-all-done.3
  85.2 3.5 %all-to-all-start.2 = ((bf16[4,176,256]{2,1,0:T(8,128)(2,1)}), bf16[4,176,256]{2,1,0:T(8,128)(2,1)S(1)}, u32[]{:S(2)}, u32[]{:S(2)}) async-start(bf16[4,176,256]{2,1,0:T(8,128)(2,1)} %bitcast.13), calls=%async_computation.2 | async-start | bytes 720896 | tf_op jit(solution)/shard_map/all_to_all | solution.py:292
  88.7 34.0 %tasks.3 = bf16[704,256]{1,0:T(8,128)(2,1)S(1)} custom-call(s32[1024]{0:T(1024)S(1)} %reshape.321.tasks_ref, s32[512]{0:T(512)S(1)} %get-tuple-element.42.slots_ref, s32[512]{0:T(512)S(1)} %get-tuple-element.29.places_ref, bf16[192,16,128]{2,1,0:T(8,128)(2,1)S(1)} %copy-done, bf16[1536,256]{1,0:T(8,128)(2,1)S(1)} %bitcast.32, ...), custom_call_target="tpu_custom_call" | custom-call | flops 34359738368 | bytes 786432 | tf_op jit(solution)/shard_map/tasks/pallas_call | solution.py:234
  122.7 0.0 all-to-all-done.2
  122.7 10.1 %all_to_all.29 = bf16[4,176,256]{2,1,0:T(8,128)(2,1)S(1)} all-to-all(bf16[4,176,256]{2,1,0:T(8,128)(2,1)S(1)} %bitcast.33), channel_id=1, replica_groups=mesh['bra'=8,'ket'=4] {'ket'}, dimensions={0} | all-to-all | bytes 720896 | tf_op jit(solution)/shard_map/all_to_all | solution.py:292
  132.9 2.7 %sum_blocks.1 = f32[1152,256]{1,0:T(8,128)S(1)} custom-call(bf16[704,256]{1,0:T(8,128)(2,1)S(1)} %bitcast.29, bf16[704,256]{1,0:T(8,128)(2,1)S(1)} %bitcast.30), custom_call_target="tpu_custom_call" | custom-call | tf_op jit(solution)/shard_map/sum_blocks/pallas_call | solution.py:280
  135.6 2.2 %copy.31 = f32[24,48,1,256]{3,2,1,0:T(1,128)} copy(f32[24,48,1,256]{3,1,0,2:T(8,128)S(1)} %bitcast.28) | data formatting | bytes 2359296 | tf_op jit(solution)/shard_map/reshape | solution.py:352
  (25 shorter events, 0.5 us)
Async XLA Ops:
  0.0 13.8 %copy-start.2 = (s32[1,1,512,4]{2,3,1,0:T(4,128)S(1)}, s32[1,1,512,4]{2,3,1,0:T(4,128)}, u32[]{:S(2)}) copy-start(s32[1,1,512,4]{2,3,1,0:T(4,128)} %param.3) | copy-start | bytes 24580
  2.2 18.5 %copy-start.1 = (bf16[24,48,1,256]{3,1,2,0:T(8,128)(2,1)S(1)}, bf16[24,48,1,256]{3,1,2,0:T(8,128)(2,1)}, u32[]{:S(2)}) copy-start(bf16[24,48,1,256]{3,1,2,0:T(8,128)(2,1)} %param.5) | copy-start | bytes 1769476
  6.5 13.8 %all-to-all-start = ((s32[8,1,384]{2,1,0:T(1,128)}), s32[8,1,384]{2,1,0:T(1,128)S(1)}, u32[]{:S(2)}, u32[]{:S(2)}) async-start(s32[8,1,384]{2,1,0:T(1,128)} %bitcast.4), calls=%async_computation | async-start | bytes 24576 | tf_op jit(solution)/shard_map/all_to_all | solution.py:292
  24.3 22.6 %all-to-all-start.1 = ((bf16[8,192,256]{2,1,0:T(8,128)(2,1)}), bf16[8,192,256]{2,1,0:T(8,128)(2,1)S(1)}, u32[]{:S(2)}, u32[]{:S(2)}) async-start(bf16[8,192,256]{2,1,0:T(8,128)(2,1)} %bitcast.11), calls=%async_computation.1 | async-start | bytes 1572864 | tf_op jit(solution)/shard_map/all_to_all | solution.py:292
  33.7 16.8 %copy-start = (bf16[192,16,128]{2,1,0:T(8,128)(2,1)S(1)}, bf16[192,16,128]{2,1,0:T(8,128)(2,1)}, u32[]{:S(2)}) copy-start(bf16[192,16,128]{2,1,0:T(8,128)(2,1)} %fac_ref.3) | copy-start | bytes 2359300
  46.9 38.3 %all-to-all-start.3 = ((bf16[8,192,256]{2,1,0:T(8,128)(2,1)}), bf16[8,192,256]{2,1,0:T(8,128)(2,1)S(1)}, u32[]{:S(2)}, u32[]{:S(2)}) async-start(bf16[8,192,256]{2,1,0:T(8,128)(2,1)} %bitcast.15), calls=%async_computation.3 | async-start | bytes 1572864 | tf_op jit(solution)/shard_map/all_to_all | solution.py:292
  85.2 37.5 %all-to-all-start.2 = ((bf16[4,176,256]{2,1,0:T(8,128)(2,1)}), bf16[4,176,256]{2,1,0:T(8,128)(2,1)S(1)}, u32[]{:S(2)}, u32[]{:S(2)}) async-start(bf16[4,176,256]{2,1,0:T(8,128)(2,1)} %bitcast.13), calls=%async_computation.2 | async-start | bytes 720896 | tf_op jit(solution)/shard_map/all_to_all | solution.py:292

commit v4 on v3

--- a/solution.py
+++ b/solution.py
@@ -28,89 +28,154 @@
     return jnp.where(mask, 1.0, 0.0).astype(jnp.bfloat16)
 
 
-def plan_kernel(sides, bucket_refs, wanted_refs, slot_refs, asked_refs):
-    items = bucket_refs[0].shape[1]
+def slots_of(bucket, upper, buckets, capacity):
+    owner_id = iota((buckets, bucket.shape[1]), 0)
+    marked = jnp.where(bucket == owner_id, 1.0, 0.0)
+    counted = dot(marked.astype(jnp.bfloat16), upper, NN)
+    offset = (owner_id * capacity - 1).astype(jnp.float32)
+    return jnp.sum(marked * (counted + offset), axis=0, keepdims=True).astype(jnp.int32)
+
+
+def split_values(wanted):
+    which = iota((16, wanted.shape[1]), 0)
+    values = jnp.where(which == 0, wanted >> 6, jnp.where(which == 1, wanted & 63, 0))
+    return values.astype(jnp.float32).astype(jnp.bfloat16)
+
+
+def listed(slot, values, first, width):
+    picked = hot(slot == iota((width, slot.shape[1]), 0) + first)
+    found = dot(values, picked, NT)
+    return (found[0:1] * 64.0 + found[1:2]).astype(jnp.int32)
+
+
+def front_kernel(
+    bra_bucket, bra_wanted, ket_bucket, ket_wanted, table_ref,
+    bra_slot, ket_slot, ket_asked, got_out, later_out,
+    asked, heard, answer, got, ask_send, ask_recv, ans_send, ans_recv,
+    *, peers, cap_bra, kets, cap_ket,
+):
+    me = lax.axis_index("bra")
+    barrier = pltpu.get_barrier_semaphore()
+    for k in range(1, peers):
+        pl.semaphore_signal(
+            barrier, inc=1, device_id={"bra": lax.rem(me + k, peers)},
+            device_id_type=pl.DeviceIdType.MESH,
+        )
+    items = bra_bucket.shape[1]
+    width = asked.shape[2]
+    blocks = table_ref.shape[0]
     upper = hot(iota((items, items), 0) <= iota((items, items), 1))
-    for side, (buckets, capacity) in enumerate(sides):
-        owner_id = iota((buckets, items), 0)
-        marked = jnp.where(bucket_refs[side][...] == owner_id, 1.0, 0.0)
-        counted = dot(marked.astype(jnp.bfloat16), upper, NN)
-        offset = (owner_id * capacity - 1).astype(jnp.float32)
-        slot = jnp.sum(marked * (counted + offset), axis=0, keepdims=True).astype(jnp.int32)
-        slot_refs[side][...] = slot
-        wanted = wanted_refs[side][...]
-        which = iota((16, items), 0)
-        high, low = wanted >> 6, wanted & 63
-        values = jnp.where(which == 0, high, jnp.where(which == 1, low, 0))
-        values = values.astype(jnp.float32).astype(jnp.bfloat16)
-        width = 256
-
-        def part(k, carry, side=side, slot=slot, values=values):
-            first = pl.multiple_of(k * width, width)
-            picked = hot(slot == iota((width, items), 0) + first)
-            found = dot(values, picked, NT)
-            asked_refs[side][:, pl.ds(first, width)] = (
-                found[0:1] * 64.0 + found[1:2]
-            ).astype(jnp.int32)
-            return carry
-
-        lax.fori_loop(0, buckets * capacity // width, part, 0)
-
-
-def plan(buckets, wanted, sides):
-    count = len(sides)
-    items = buckets[0].shape[1]
-
-    def kernel(*refs):
-        plan_kernel(
-            sides,
-            refs[:count],
-            refs[count : 2 * count],
-            refs[2 * count : 3 * count],
-            refs[3 * count :],
+    slot = slots_of(bra_bucket[...], upper, 2 * peers, cap_bra)
+    slot_k = slots_of(ket_bucket[...], upper, 2 * kets, cap_ket)
+    bra_slot[...] = slot
+    ket_slot[...] = slot_k
+    values = split_values(bra_wanted[...])
+
+    def ask_list(p, carry):
+        ids = listed(slot, values, p * (2 * cap_bra), width)
+        asked[p] = jnp.broadcast_to(ids, asked.shape[1:])
+        return carry
+
+    lax.fori_loop(0, peers, ask_list, 0)
+
+    def ask(k):
+        peer = lax.rem(me + k, peers)
+        return pltpu.make_async_remote_copy(
+            src_ref=asked.at[peer], dst_ref=heard.at[me],
+            send_sem=ask_send.at[k], recv_sem=ask_recv.at[k],
+            device_id={"bra": peer}, device_id_type=pl.DeviceIdType.MESH,
         )
 
-    out = pl.pallas_call(
-        kernel,
-        out_shape=[jax.ShapeDtypeStruct((1, items), jnp.int32)] * count
-        + [jax.ShapeDtypeStruct((1, b * c), jnp.int32) for b, c in sides],
-        in_specs=[VMEM] * (2 * count),
-        out_specs=[VMEM] * (2 * count),
-        compiler_params=PARAMS,
-        name="plan",
-    )(*buckets, *wanted)
-    return out[:count], out[count:]
-
-
-def serve_kernel(ids_ref, table_ref, out_ref):
-    rows = ids_ref.shape[1]
-    blocks = table_ref.shape[0]
-    spread = jnp.broadcast_to(ids_ref[...], (128, rows)).T
-    spread = jnp.concatenate([spread] * (blocks // 128), axis=1)
-    picked = hot(spread == iota((rows, blocks), 1))
-    out_ref[...] = dot(picked, table_ref[...], NN).astype(jnp.bfloat16)
-
-
-def serve(ids, table):
-    wide = 256
-    total = ids.shape[1]
+    def give(k):
+        peer = lax.rem(me + peers - k, peers)
+        return pltpu.make_async_remote_copy(
+            src_ref=answer.at[peer], dst_ref=got.at[me],
+            send_sem=ans_send.at[k], recv_sem=ans_recv.at[k],
+            device_id={"bra": peer}, device_id_type=pl.DeviceIdType.MESH,
+        )
+
+    def serve(ids, which):
+        spread = jnp.broadcast_to(ids[0:1], (128, width)).T
+        spread = spread[which * cap_bra : (which + 1) * cap_bra]
+        spread = jnp.concatenate([spread] * (blocks // 128), axis=1)
+        picked = hot(spread == iota((cap_bra, blocks), 1))
+        return dot(picked, table_ref[...], NN).astype(jnp.bfloat16)
+
+    pl.semaphore_wait(barrier, peers - 1)
+
+    def send_ask(k, carry):
+        ask(k).start()
+        return carry
+
+    lax.fori_loop(1, peers, send_ask, 0)
+    got[me] = serve(asked[me], 0)
+    later_out[me] = serve(asked[me], 1)
+
+    def reply(k, carry):
+        ask(k).wait_recv()
+        peer = lax.rem(me + peers - k, peers)
+        answer[peer] = serve(heard[peer], 0)
+        give(k).start()
+        return carry
+
+    lax.fori_loop(1, peers, reply, 0)
+
+    def reply_later(k, carry):
+        peer = lax.rem(me + peers - k, peers)
+        later_out[peer] = serve(heard[peer], 1)
+        return carry
+
+    lax.fori_loop(1, peers, reply_later, 0)
+    values_k = split_values(ket_wanted[...])
+    part = 256
+
+    def place_list(k, carry):
+        first = pl.multiple_of(k * part, part)
+        ket_asked[:, pl.ds(first, part)] = listed(slot_k, values_k, first, part)
+        return carry
+
+    lax.fori_loop(0, ket_asked.shape[1] // part, place_list, 0)
+
+    def finish(k, carry):
+        ask(k).wait_send()
+        give(k).wait_send()
+        give(k).wait_recv()
+        return carry
+
+    lax.fori_loop(1, peers, finish, 0)
+    got_out[...] = got[...]
+
+
+def front(bra_bucket, bra_wanted, ket_bucket, ket_wanted, table, peers, cap_bra, kets, cap_ket):
+    items = bra_bucket.shape[1]
+    width = -(-2 * cap_bra // 128) * 128
+    size = table.shape[1]
+    blocks = (peers, cap_bra, size)
     return pl.pallas_call(
-        serve_kernel,
-        grid=(total // wide,),
-        out_shape=jax.ShapeDtypeStruct((total, table.shape[1]), jnp.bfloat16),
-        in_specs=[
-            pl.BlockSpec((1, wide), lambda k: (0, k)),
-            pl.BlockSpec(table.shape, lambda k: (0, 0)),
+        functools.partial(
+            front_kernel, peers=peers, cap_bra=cap_bra, kets=kets, cap_ket=cap_ket
+        ),
+        out_shape=[
+            jax.ShapeDtypeStruct((1, items), jnp.int32),
+            jax.ShapeDtypeStruct((1, items), jnp.int32),
+            jax.ShapeDtypeStruct((1, 2 * kets * cap_ket), jnp.int32),
+            jax.ShapeDtypeStruct(blocks, jnp.bfloat16),
+            jax.ShapeDtypeStruct(blocks, jnp.bfloat16),
         ],
-        out_specs=pl.BlockSpec((wide, table.shape[1]), lambda k: (k, 0)),
-        compiler_params=PARAMS,
-        cost_estimate=pl.CostEstimate(
-            flops=2 * total * table.shape[0] * table.shape[1],
-            bytes_accessed=4 * total * table.shape[1],
-            transcendentals=0,
+        in_specs=[VMEM] * 5,
+        out_specs=[VMEM] * 5,
+        scratch_shapes=[
+            pltpu.VMEM((peers, 8, width), jnp.int32),
+            pltpu.VMEM((peers, 8, width), jnp.int32),
+            pltpu.VMEM(blocks, jnp.bfloat16),
+            pltpu.VMEM(blocks, jnp.bfloat16),
+        ]
+        + [pltpu.SemaphoreType.DMA((peers,))] * 4,
+        compiler_params=pltpu.CompilerParams(
+            vmem_limit_bytes=48 * 1024 * 1024, collective_id=0, has_side_effects=True
         ),
-        name="serve",
-    )(ids, table)
+        name="front",
+    )(bra_bucket, bra_wanted, ket_bucket, ket_wanted, table)
 
 
 def pair_rows(slow_ref, slow, fast):
@@ -150,7 +215,7 @@
         spread[f] = dot(dens_jd, hot((row_hi == col_lo) & (row_lo == f)), NN)
         return carry
 
-    lax.fori_loop(0, funcs, spread_one, 0, unroll=4)
+    lax.fori_loop(0, funcs, spread_one, 0, unroll=8)
 
     def form(t, raw_ref, k):
         shell_i, shell_j = tasks_ref[4 * t], tasks_ref[4 * t + 1]
@@ -208,7 +273,7 @@
         dens[1] += dot(rows, hot((row_hi == col_hi) & (col_lo == e)), NN)
         return carry
 
-    lax.fori_loop(0, funcs, fold, 0, unroll=4)
+    lax.fori_loop(0, funcs, fold, 0, unroll=8)
     dens[1] = dens[1] * (-0.5 * tile_scale)
     routed[...] = jnp.zeros_like(routed)
     owners = ids_ref.shape[0] // 2
@@ -311,17 +376,11 @@
     target = jnp.stack([shell_j, shell_c], axis=1).reshape(-1)
     position = jnp.repeat(shell_i % rows_per_device, 2) * cols_dev + target // ket_count
     ket_bucket = target % ket_count * 2 + half_of
-    slot_bra, asked_bra = plan(
-        [bra_bucket[None]], [wanted[None]], ((2 * bra_count, cap_bra),)
+    slot_bra, slot_ket, asked_ket, first_got, later = front(
+        bra_bucket[None], wanted[None], ket_bucket[None], position[None], table,
+        bra_count, cap_bra, ket_count, cap_ket,
     )
-    asked_bra = trade(asked_bra[0].reshape(bra_count, 2 * cap_bra), "bra")
-    asked_bra = asked_bra.reshape(bra_count, 2, cap_bra).transpose(1, 0, 2)
-    served = [serve(asked_bra[which].reshape(1, -1), table) for which in range(2)]
-    late_bucket, served[0] = lax.optimization_barrier((ket_bucket, served[0]))
-    slot_ket, asked_ket = plan(
-        [late_bucket[None]], [position[None]], ((2 * ket_count, cap_ket),)
-    )
-    slots = (slot_bra[0], slot_ket[0])
+    slots = (slot_bra, slot_ket)
 
     def per_half(slot, capacity, stride, which):
         bucket, place = slot // capacity, slot % capacity
@@ -329,13 +388,13 @@
         return local[which * task_count : (which + 1) * task_count]
 
     stride = cap_ket + id_rows
-    ids = asked_ket[0].reshape(ket_count, 2, cap_ket)
+    ids = asked_ket.reshape(ket_count, 2, cap_ket)
     ids = jnp.stack([ids >> 6, ids & 63], axis=2).astype(jnp.float32)
     ids = jnp.pad(ids, ((0, 0), (0, 0), (0, 0), (0, size - cap_ket)), constant_values=-1.0)
 
     results = []
     for which in range(2):
-        got = trade(served[which].reshape(bra_count, cap_bra, size), "bra")
+        got = first_got if which == 0 else trade(later, "bra")
         outgoing = run_tasks(
             quartets[which * half : (which + 1) * half].reshape(-1),
             per_half(slots[0].reshape(-1), cap_bra, cap_bra, which),

time: 138 us -> 124 us (0.90)
  waiting for transfers between devices: 18.2 us -> 0.01 us
  Pallas kernels: 84.7 us -> 99.4 us
  starting transfers between devices: 17.8 us -> 7.22 us
    all_to_all x4 -> x2, waiting for transfers between devices: 18.2 us -> 0.01 us  [trade(): return lax.all_to_all(array, axis, split_axis=0, concat_axis=0, tiled=True)]
    pallas_call x4 -> x1, Pallas kernels: 13.2 us -> 29.4 us  [front(): pl.pallas_call(functools.partial(front_kernel, peers=peers, cap_bra=cap_b...]
    all_to_all x4 -> x2, starting transfers between devices: 17.8 us -> 7.22 us  [trade(): return lax.all_to_all(array, axis, split_axis=0, concat_axis=0, tiled=True)]
  transfers between devices with their start and end apart: 4 -> 2, of which waited for: 2 -> 0; matrix products, arithmetic and copies ran while one was open for 1% -> 1% of each run, Pallas kernels for 54% -> 54%
where the time goes in v4:
time: 124 us
  Pallas kernels  99.4 us (80%)
  blocking collectives  10.2 us (8%)
  starting transfers between devices  7.22 us (6%)
  local copies, waits for them, and re-layouts  5.66 us (5%)
    pallas_call x2, Pallas kernels, run_tasks(): pl.pallas_call(functools.partial(task_kernel, unroll=unroll), out_shape=j...  67.4 us
    pallas_call x1, Pallas kernels, front(): pl.pallas_call(functools.partial(front_kernel, peers=peers, cap_bra=cap_b...  29.4 us
    all_to_all x1, blocking collectives, trade(): return lax.all_to_all(array, axis, split_axis=0, concat_axis=0, tiled=True)  10.2 us
    all_to_all x2, starting transfers between devices, trade(): return lax.all_to_all(array, axis, split_axis=0, concat_axis=0, tiled=True)  7.22 us
    pallas_call x1, Pallas kernels, sum_blocks(): pl.pallas_call(functools.partial(sum_kernel, sources=sources), grid=(tota...  2.67 us
  transfers between devices with their start and end apart: 2, of which 0 were waited for; matrix products, arithmetic and copies ran while one was open for 1% of the time, Pallas kernels for 54%

profile of v4, /device:TPU:0, one launch (start us, length us, event | category | flops | bytes accessed | tf_op | source)
XLA Modules:
  0.0 123.9 jit_solution(6449248044034639769)
XLA Ops:
  0.0 0.9 slice_remainder_fusion
  0.9 0.7 stack.14
  1.6 0.1 broadcast_in_dim.4
  1.8 0.2 reshape.335
  1.9 0.0 copy-start
  1.9 0.1 copy.13
  2.1 0.2 rem.156
  2.3 0.1 copy.14
  2.4 0.2 div.83
  2.6 0.2 copy.12
  2.8 0.2 ne.217
  3.0 0.1 broadcast_in_dim.5
  3.2 0.2 mul.56
  3.3 0.1 copy.15
  3.5 0.2 reshape.336
  3.7 0.0 copy-start.2
  3.8 0.0 copy-done
  3.8 29.4 %front.1 = (s32[1,1024]{1,0:T(1,128)S(1)}, s32[1,1024]{1,0:T(1,128)S(1)}, s32[1,1280]{1,0:T(1,128)S(1)}, bf16[8,192,256]{2,1,0:T(8,128)(2,1)S(1)}, bf16[8,192,256]{2,1,0:T(8,128)(2,1)}) custom-call(s32[1,1024]{1,0:T(1,128)S(1)} %get-tuple-element.36.bra_bucket, s32[1,1024]{1,0:T(1,128)S(1)} %get-tuple-element.35.bra_wanted, ...), custom_call_target="tpu_custom_call" | custom-call | tf_op jit(solution)/shard_map/front/pallas_call | solution.py:154
  33.2 0.0 copy-start.1
  33.2 3.8 %all-to-all-start.1 = ((bf16[8,192,256]{2,1,0:T(8,128)(2,1)}), bf16[8,192,256]{2,1,0:T(8,128)(2,1)S(1)}, u32[]{:S(2)}, u32[]{:S(2)}) async-start(bf16[8,192,256]{2,1,0:T(8,128)(2,1)} %get-tuple-element.14), calls=%async_computation.1 | async-start | bytes 1572864 | tf_op jit(solution)/shard_map/all_to_all | solution.py:357
  36.9 0.0 copy-done.2
  37.0 0.1 copy.11
  37.2 0.1 reshape.333.tasks_ref
  37.4 0.1 and.149
  37.5 0.1 shift_right_arithmetic.18
  37.6 0.0 copy-done.1
  37.7 34.1 %tasks.2 = bf16[704,256]{1,0:T(8,128)(2,1)} custom-call(s32[1024]{0:T(1024)S(1)} %reshape.333.tasks_ref, s32[512]{0:T(512)S(1)} %get-tuple-element.28.slots_ref, s32[512]{0:T(512)S(1)} %get-tuple-element.26.places_ref, bf16[192,16,128]{2,1,0:T(8,128)(2,1)S(1)} %copy-done.1, bf16[1536,256]{1,0:T(8,128)(2,1)S(1)} %bitcast.29, f32[8,256]{1,0:T(8,128)S(1)} %reshape_squeeze.6.ids_ref), custom_call_target="tpu_custom_call" | custom-call | flops 34359738368 | bytes 786432 | tf_op jit(solution)/shard_map/tasks/pallas_call | solution.py:299
  71.7 0.1 copy.18
  71.9 0.1 reshape.341.tasks_ref
  72.0 0.0 all-to-all-done.1
  72.0 3.5 %all-to-all-start = ((bf16[4,176,256]{2,1,0:T(8,128)(2,1)}), bf16[4,176,256]{2,1,0:T(8,128)(2,1)S(1)}, u32[]{:S(2)}, u32[]{:S(2)}) async-start(bf16[4,176,256]{2,1,0:T(8,128)(2,1)} %bitcast.9), calls=%async_computation | async-start | bytes 720896 | tf_op jit(solution)/shard_map/all_to_all | solution.py:357
  75.5 33.3 %tasks.3 = bf16[704,256]{1,0:T(8,128)(2,1)S(1)} custom-call(s32[1024]{0:T(1024)S(1)} %reshape.341.tasks_ref, s32[512]{0:T(512)S(1)} %get-tuple-element.27.slots_ref, s32[512]{0:T(512)S(1)} %get-tuple-element.25.places_ref, bf16[192,16,128]{2,1,0:T(8,128)(2,1)S(1)} %copy-done.1, bf16[1536,256]{1,0:T(8,128)(2,1)S(1)} %bitcast.26, ...), custom_call_target="tpu_custom_call" | custom-call | flops 34359738368 | bytes 786432 | tf_op jit(solution)/shard_map/tasks/pallas_call | solution.py:299
  108.9 0.0 all-to-all-done
  108.9 10.2 %all_to_all.15 = bf16[4,176,256]{2,1,0:T(8,128)(2,1)S(1)} all-to-all(bf16[4,176,256]{2,1,0:T(8,128)(2,1)S(1)} %bitcast.28), channel_id=1, replica_groups=mesh['bra'=8,'ket'=4] {'ket'}, dimensions={0} | all-to-all | bytes 720896 | tf_op jit(solution)/shard_map/all_to_all | solution.py:357
  119.0 2.7 %sum_blocks.1 = f32[1152,256]{1,0:T(8,128)S(1)} custom-call(bf16[704,256]{1,0:T(8,128)(2,1)S(1)} %bitcast.24, bf16[704,256]{1,0:T(8,128)(2,1)S(1)} %bitcast.25), custom_call_target="tpu_custom_call" | custom-call | tf_op jit(solution)/shard_map/sum_blocks/pallas_call | solution.py:345
  121.7 2.2 %copy.19 = f32[24,48,1,256]{3,2,1,0:T(1,128)} copy(f32[24,48,1,256]{3,1,0,2:T(8,128)S(1)} %bitcast.23) | data formatting | bytes 2359296 | tf_op jit(solution)/shard_map/reshape | solution.py:411
  (20 shorter events, 0.3 us)
Async XLA Ops:
  1.9 1.8 %copy-start = (bf16[24,48,1,256]{3,1,2,0:T(8,128)(2,1)S(1)}, bf16[24,48,1,256]{3,1,2,0:T(8,128)(2,1)}, u32[]{:S(2)}) copy-start(bf16[24,48,1,256]{3,1,2,0:T(8,128)(2,1)} %param.5) | copy-start | bytes 1769476
  3.7 33.2 %copy-start.2 = (s32[1,1,512,4]{2,3,1,0:T(4,128)S(1)}, s32[1,1,512,4]{2,3,1,0:T(4,128)}, u32[]{:S(2)}) copy-start(s32[1,1,512,4]{2,3,1,0:T(4,128)} %param.3) | copy-start | bytes 24580
  33.2 4.5 %copy-start.1 = (bf16[192,16,128]{2,1,0:T(8,128)(2,1)S(1)}, bf16[192,16,128]{2,1,0:T(8,128)(2,1)}, u32[]{:S(2)}) copy-start(bf16[192,16,128]{2,1,0:T(8,128)(2,1)} %fac_ref.3) | copy-start | bytes 2359300
  33.2 38.8 %all-to-all-start.1 = ((bf16[8,192,256]{2,1,0:T(8,128)(2,1)}), bf16[8,192,256]{2,1,0:T(8,128)(2,1)S(1)}, u32[]{:S(2)}, u32[]{:S(2)}) async-start(bf16[8,192,256]{2,1,0:T(8,128)(2,1)} %get-tuple-element.14), calls=%async_computation.1 | async-start | bytes 1572864 | tf_op jit(solution)/shard_map/all_to_all | solution.py:357
  72.0 36.8 %all-to-all-start = ((bf16[4,176,256]{2,1,0:T(8,128)(2,1)}), bf16[4,176,256]{2,1,0:T(8,128)(2,1)S(1)}, u32[]{:S(2)}, u32[]{:S(2)}) async-start(bf16[4,176,256]{2,1,0:T(8,128)(2,1)} %bitcast.9), calls=%async_computation | async-start | bytes 720896 | tf_op jit(solution)/shard_map/all_to_all | solution.py:357

commit v5 on v4

--- a/solution.py
+++ b/solution.py
@@ -322,35 +322,70 @@
     )(tasks, slots, places, factors, got, ids)
 
 
-def sum_kernel(block_a, block_b, out_ref, *, sources):
-    rows = out_ref.shape[0]
-    stride = block_a.shape[0] // sources
-    first = pl.program_id(0) * rows
-    here = (iota((rows, stride), 0) + first).astype(jnp.float32)
-    total = None
-    for block in (block_a, block_b):
-        for source in range(sources):
-            held = block[source * stride : (source + 1) * stride, :]
-            ids = held[stride - id_rows :, :].astype(jnp.float32)
-            index = (ids[0:1] * 64.0 + ids[1:2])[:, :stride]
-            term = dot(hot(jnp.broadcast_to(index, here.shape) == here), held, NN)
-            total = term if total is None else total + term
-    out_ref[...] = total
-
-
-def sum_blocks(blocks, sources, total):
+def sum_kernel(block_a, own_b, out_ref, got, sent, arrived, *, sources):
+    me = lax.axis_index("ket")
+    barrier = pltpu.get_barrier_semaphore()
+    for k in range(1, sources):
+        pl.semaphore_signal(
+            barrier, inc=1, device_id={"ket": lax.rem(me + k, sources)},
+            device_id_type=pl.DeviceIdType.MESH,
+        )
+    pl.semaphore_wait(barrier, sources - 1)
+    copies = []
+    for k in range(1, sources):
+        peer = lax.rem(me + k, sources)
+        copies.append(
+            pltpu.make_async_remote_copy(
+                src_ref=own_b.at[peer], dst_ref=got.at[k],
+                send_sem=sent.at[k], recv_sem=arrived.at[k],
+                device_id={"ket": peer}, device_id_type=pl.DeviceIdType.MESH,
+            )
+        )
+        copies[-1].start()
     rows = 128
-    size = blocks[0].shape[1]
-    whole = lambda array: pl.BlockSpec(array.shape, lambda k: (0, 0))
+    stride = block_a.shape[1]
+
+    def add(pairs, start):
+        def chunk(at, carry):
+            first = pl.multiple_of(at * rows, rows)
+            here = (iota((rows, stride), 0) + first).astype(jnp.float32)
+            place = pl.ds(first, rows)
+            total = None if start else out_ref[place, :]
+            for read in pairs:
+                held = read()
+                ids = held[stride - id_rows :, :].astype(jnp.float32)
+                index = (ids[0:1] * 64.0 + ids[1:2])[:, :stride]
+                term = dot(hot(jnp.broadcast_to(index, here.shape) == here), held, NN)
+                total = term if total is None else total + term
+            out_ref[place, :] = total
+            return carry
+
+        lax.fori_loop(0, out_ref.shape[0] // rows, chunk, 0)
+
+    early = [functools.partial(lambda k: block_a[k], k) for k in range(sources)]
+    add(early + [lambda: own_b[me]], True)
+    for copy in copies:
+        copy.wait()
+    add([functools.partial(lambda k: got[k], k) for k in range(1, sources)], False)
+
+
+def sum_blocks(block_a, own_b, total):
+    sources, stride, size = block_a.shape
     return pl.pallas_call(
         functools.partial(sum_kernel, sources=sources),
-        grid=(total // rows,),
         out_shape=jax.ShapeDtypeStruct((total, size), jnp.float32),
-        in_specs=[whole(blocks[0]), whole(blocks[1])],
-        out_specs=pl.BlockSpec((rows, size), lambda k: (k, 0)),
-        compiler_params=PARAMS,
+        in_specs=[VMEM, VMEM],
+        out_specs=VMEM,
+        scratch_shapes=[
+            pltpu.VMEM((sources, stride, size), jnp.bfloat16),
+            pltpu.SemaphoreType.DMA((sources,)),
+            pltpu.SemaphoreType.DMA((sources,)),
+        ],
+        compiler_params=pltpu.CompilerParams(
+            vmem_limit_bytes=48 * 1024 * 1024, collective_id=1, has_side_effects=True
+        ),
         name="sum_blocks",
-    )(*blocks)
+    )(block_a, own_b)
 
 
 def trade(array, axis):
@@ -405,9 +440,9 @@
             ket_count * stride,
             4,
         )
-        back = trade(outgoing.reshape(ket_count, stride, size), "ket")
-        results.append(back.reshape(-1, size))
-    fock = sum_blocks(results, ket_count, rows_per_device * cols_dev)
+        outgoing = outgoing.reshape(ket_count, stride, size)
+        results.append(trade(outgoing, "ket") if which == 0 else outgoing)
+    fock = sum_blocks(results[0], results[1], rows_per_device * cols_dev)
     return fock.reshape(rows_per_device, cols_dev, 1, size)
 
 

time: 124 us -> 120 us (0.968)
  blocking collectives: 10.2 us -> 0 us
  Pallas kernels: 99.4 us -> 105 us
    all_to_all x1 -> x0, blocking collectives: 10.2 us -> none  [trade(): return lax.all_to_all(array, axis, split_axis=0, concat_axis=0, tiled=True)]
    pallas_call x1, Pallas kernels: 2.67 us -> 8.3 us  [sum_blocks(): pl.pallas_call(functools.partial(sum_kernel, sources=sources), out_shape=...]
  transfers between devices with their start and end apart: 2 -> 2, of which waited for: 0 -> 0; matrix products, arithmetic and copies ran while one was open for 1% -> 1% of each run, Pallas kernels for 54% -> 56%
where the time goes in v5:
time: 120 us; the launch traced here: 119 us
  Pallas kernels  105 us (88%)
  starting transfers between devices  7.22 us (6%)
  local copies, waits for them, and re-layouts  5.66 us (5%)
    pallas_call x2, Pallas kernels, run_tasks(): pl.pallas_call(functools.partial(task_kernel, unroll=unroll), out_shape=j...  67.5 us
    pallas_call x1, Pallas kernels, front(): pl.pallas_call(functools.partial(front_kernel, peers=peers, cap_bra=cap_b...  29.4 us
    pallas_call x1, Pallas kernels, sum_blocks(): pl.pallas_call(functools.partial(sum_kernel, sources=sources), out_shape=...  8.3 us
    all_to_all x2, starting transfers between devices, trade(): return lax.all_to_all(array, axis, split_axis=0, concat_axis=0, tiled=True)  7.22 us
  transfers between devices with their start and end apart: 2, of which 0 were waited for; matrix products, arithmetic and copies ran while one was open for 1% of the time, Pallas kernels for 56%

profile of v5, /device:TPU:0, one launch (start us, length us, event | category | flops | bytes accessed | tf_op | source)
XLA Modules:
  0.0 119.4 jit_solution(16903876001253902463)
XLA Ops:
  0.0 0.9 slice_remainder_fusion
  0.9 0.7 stack.14
  1.6 0.1 broadcast_in_dim.4
  1.8 0.2 reshape.329
  1.9 0.0 copy-start
  1.9 0.1 copy.13
  2.1 0.2 rem.156
  2.3 0.1 copy.14
  2.4 0.2 div.83
  2.6 0.2 copy.12
  2.8 0.2 ne.217
  3.0 0.1 broadcast_in_dim.5
  3.2 0.2 mul.56
  3.3 0.1 copy.15
  3.5 0.2 reshape.330
  3.7 0.0 copy-start.2
  3.8 0.0 copy-done
  3.8 29.4 %front.1 = (s32[1,1024]{1,0:T(1,128)S(1)}, s32[1,1024]{1,0:T(1,128)S(1)}, s32[1,1280]{1,0:T(1,128)S(1)}, bf16[8,192,256]{2,1,0:T(8,128)(2,1)S(1)}, bf16[8,192,256]{2,1,0:T(8,128)(2,1)}) custom-call(s32[1,1024]{1,0:T(1,128)S(1)} %get-tuple-element.36.bra_bucket, s32[1,1024]{1,0:T(1,128)S(1)} %get-tuple-element.35.bra_wanted, ...), custom_call_target="tpu_custom_call" | custom-call | tf_op jit(solution)/shard_map/front/pallas_call | solution.py:154
  33.2 0.0 copy-start.1
  33.2 3.8 %all-to-all-start.1 = ((bf16[8,192,256]{2,1,0:T(8,128)(2,1)}), bf16[8,192,256]{2,1,0:T(8,128)(2,1)S(1)}, u32[]{:S(2)}, u32[]{:S(2)}) async-start(bf16[8,192,256]{2,1,0:T(8,128)(2,1)} %get-tuple-element.14), calls=%async_computation.1 | async-start | bytes 1572864 | tf_op jit(solution)/shard_map/all_to_all | solution.py:392
  36.9 0.0 copy-done.2
  37.0 0.1 copy.11
  37.2 0.1 reshape.327.tasks_ref
  37.4 0.1 and.149
  37.5 0.1 shift_right_arithmetic.18
  37.6 0.0 copy-done.1
  37.7 34.1 %tasks.2 = bf16[704,256]{1,0:T(8,128)(2,1)} custom-call(s32[1024]{0:T(1024)S(1)} %reshape.327.tasks_ref, s32[512]{0:T(512)S(1)} %get-tuple-element.28.slots_ref, s32[512]{0:T(512)S(1)} %get-tuple-element.26.places_ref, bf16[192,16,128]{2,1,0:T(8,128)(2,1)S(1)} %copy-done.1, bf16[1536,256]{1,0:T(8,128)(2,1)S(1)} %bitcast.25, f32[8,256]{1,0:T(8,128)S(1)} %reshape_squeeze.6.ids_ref), custom_call_target="tpu_custom_call" | custom-call | flops 34359738368 | bytes 786432 | tf_op jit(solution)/shard_map/tasks/pallas_call | solution.py:299
  71.8 0.1 copy.18
  71.9 0.1 reshape.334.tasks_ref
  72.0 0.0 all-to-all-done.1
  72.0 3.5 %all-to-all-start = ((bf16[4,176,256]{2,1,0:T(8,128)(2,1)}), bf16[4,176,256]{2,1,0:T(8,128)(2,1)S(1)}, u32[]{:S(2)}, u32[]{:S(2)}) async-start(bf16[4,176,256]{2,1,0:T(8,128)(2,1)} %bitcast.9), calls=%async_computation | async-start | bytes 720896 | tf_op jit(solution)/shard_map/all_to_all | solution.py:392
  75.5 33.4 %tasks.3 = bf16[704,256]{1,0:T(8,128)(2,1)S(1)} custom-call(s32[1024]{0:T(1024)S(1)} %reshape.334.tasks_ref, s32[512]{0:T(512)S(1)} %get-tuple-element.27.slots_ref, s32[512]{0:T(512)S(1)} %get-tuple-element.25.places_ref, bf16[192,16,128]{2,1,0:T(8,128)(2,1)S(1)} %copy-done.1, bf16[1536,256]{1,0:T(8,128)(2,1)S(1)} %bitcast.22, ...), custom_call_target="tpu_custom_call" | custom-call | flops 34359738368 | bytes 786432 | tf_op jit(solution)/shard_map/tasks/pallas_call | solution.py:299
  108.9 0.0 all-to-all-done.block_a
  108.9 8.3 %sum_blocks.1 = f32[1152,256]{1,0:T(8,128)S(1)} custom-call(bf16[4,176,256]{2,1,0:T(8,128)(2,1)S(1)} %all-to-all-done.block_a, bf16[4,176,256]{2,1,0:T(8,128)(2,1)S(1)} %bitcast.24), custom_call_target="tpu_custom_call" | custom-call | tf_op jit(solution)/shard_map/sum_blocks/pallas_call | solution.py:374
  117.2 2.2 %copy.19 = f32[24,48,1,256]{3,2,1,0:T(1,128)} copy(f32[24,48,1,256]{3,1,0,2:T(8,128)S(1)} %bitcast.21) | data formatting | bytes 2359296 | tf_op jit(solution)/shard_map/reshape | solution.py:446
  (20 shorter events, 0.3 us)
Async XLA Ops:
  1.9 1.8 %copy-start = (bf16[24,48,1,256]{3,1,2,0:T(8,128)(2,1)S(1)}, bf16[24,48,1,256]{3,1,2,0:T(8,128)(2,1)}, u32[]{:S(2)}) copy-start(bf16[24,48,1,256]{3,1,2,0:T(8,128)(2,1)} %param.5) | copy-start | bytes 1769476
  3.7 33.2 %copy-start.2 = (s32[1,1,512,4]{2,3,1,0:T(4,128)S(1)}, s32[1,1,512,4]{2,3,1,0:T(4,128)}, u32[]{:S(2)}) copy-start(s32[1,1,512,4]{2,3,1,0:T(4,128)} %param.3) | copy-start | bytes 24580
  33.2 4.5 %copy-start.1 = (bf16[192,16,128]{2,1,0:T(8,128)(2,1)S(1)}, bf16[192,16,128]{2,1,0:T(8,128)(2,1)}, u32[]{:S(2)}) copy-start(bf16[192,16,128]{2,1,0:T(8,128)(2,1)} %fac_ref.3) | copy-start | bytes 2359300
  33.2 38.9 %all-to-all-start.1 = ((bf16[8,192,256]{2,1,0:T(8,128)(2,1)}), bf16[8,192,256]{2,1,0:T(8,128)(2,1)S(1)}, u32[]{:S(2)}, u32[]{:S(2)}) async-start(bf16[8,192,256]{2,1,0:T(8,128)(2,1)} %get-tuple-element.14), calls=%async_computation.1 | async-start | bytes 1572864 | tf_op jit(solution)/shard_map/all_to_all | solution.py:392
  72.0 36.8 %all-to-all-start = ((bf16[4,176,256]{2,1,0:T(8,128)(2,1)}), bf16[4,176,256]{2,1,0:T(8,128)(2,1)S(1)}, u32[]{:S(2)}, u32[]{:S(2)}) async-start(bf16[4,176,256]{2,1,0:T(8,128)(2,1)} %bitcast.9), calls=%async_computation | async-start | bytes 720896 | tf_op jit(solution)/shard_map/all_to_all | solution.py:392
